TPU v7x, 256 devices: a whole 4x4x8 slice. The times are simulated.
256 devices in a mesh: ia: 8 (over x, y_lo), ja: 4 (over y_hi, core), ka: 8 (over z).
Axes of the slice: x: 4, y: 4 (y_hi: 2, y_lo: 2; y = y_hi * 2 + y_lo), z: 8, core: 2. Of those that a mesh axis runs over, the one named last changes fastest.
Arguments:
- pre_act: bfloat16 [4096, 24576], P('ia', ('ja', 'ka')), may hold values from -6 to 6
- down_weight: bfloat16 [6144, 24576], P(('ka', 'ia'), 'ja'), may hold values from -0.109375 to 0.109375
- grad_out: bfloat16 [4096, 6144], P('ia', ('ka', 'ja')), may hold values from -6 to 6
Outputs:
- output: bfloat16 [4096, 6144], P('ia', ('ka', 'ja'))
- grad_pre: bfloat16 [4096, 24576], P('ia', ('ja', 'ka'))
- grad_weight: bfloat16 [6144, 24576], P(('ka', 'ia'), 'ja')
All inputs are finite; a program needn't handle non-finite values.
Results may differ from a plain program's by a relative error of at most 0.02.
Values may be sent and summed in bfloat16 or wider, within the bound.
No kernel may reach another device: no remote copies, remote signals or barrier semaphores. Data moves between devices by JAX's collectives and lax.ppermute only.
A program may use at most 128 MiB of HBM per device.

v0:
```python
import jax
import jax.numpy as jnp
from jax import lax
from jax.sharding import PartitionSpec as P

coeff = 0.7978845608028654


def gelu_value(v):
    return 0.5 * v * (1.0 + jnp.tanh(coeff * (v + 0.044715 * v * v * v)))


def gelu_slope(v):
    tval = jnp.tanh(coeff * (v + 0.044715 * v * v * v))
    return 0.5 * (1.0 + tval) + 0.5 * v * (1.0 - tval * tval) * coeff * (
        1.0 + 3.0 * 0.044715 * v * v
    )


def shards(pre_act, down_weight, grad_out):
    pre32 = pre_act.astype(jnp.float32)
    pre_block = lax.all_gather(pre_act, "ka", axis=1, tiled=True)
    hidden = gelu_value(pre_block.astype(jnp.float32)).astype(jnp.bfloat16)
    grad_block = lax.all_gather(grad_out, "ja", axis=1, tiled=True)
    weight_block = lax.all_gather(down_weight, "ia", axis=0, tiled=True)
    out_terms = lax.dot_general(
        hidden, weight_block, (((1,), (1,)), ((), ())), preferred_element_type=jnp.float32
    )
    hidden_terms = jnp.dot(grad_block, weight_block, preferred_element_type=jnp.float32)
    output = lax.psum_scatter(out_terms.astype(jnp.bfloat16), "ja", scatter_dimension=1, tiled=True)
    grad_hidden = lax.psum_scatter(
        hidden_terms.astype(jnp.bfloat16), "ka", scatter_dimension=1, tiled=True
    ).astype(jnp.float32)
    grad_pre = (grad_hidden * gelu_slope(pre32)).astype(jnp.bfloat16)
    weight_terms = lax.dot_general(
        grad_block, hidden, (((0,), (0,)), ((), ())), preferred_element_type=jnp.float32
    )
    grad_weight = lax.psum_scatter(
        weight_terms.astype(jnp.bfloat16), "ia", scatter_dimension=0, tiled=True
    )
    return (output, grad_pre, grad_weight)


def solution(mesh):
    placed = (P("ia", ("ja", "ka")), P(("ka", "ia"), "ja"), P("ia", ("ka", "ja")))
    return jax.shard_map(
        shards,
        mesh=mesh,
        in_specs=placed,
        out_specs=(P("ia", ("ka", "ja")), P("ia", ("ja", "ka")), P(("ka", "ia"), "ja")),
        check_vma=False,
    )
```

profile of v0, /device:TPU:2, one launch (start us, length us, event | category | flops | bytes accessed | tf_op | source)
XLA Modules:
  0.0 595.2 jit_solution(952519811015802239)
XLA Ops:
  7.2 0.0 all-gather.5.cloned.1.call-start
  7.2 0.7 all-gather.5.cloned.1.call-update
  7.9 0.0 all-gather.3.cloned.1.call-start
  7.9 0.7 all-gather.3.cloned.1.call-update
  8.6 0.0 reduce-scatter.8.cloned.1.call-start
  8.7 10.5 %all_gather.11 = bf16[512,768]{0,1:T(8,128)(2,1)S(1)} all-gather(bf16[512,192]{0,1:T(8,128)(2,1)} %param.5), channel_id=1, replica_groups=mesh['ia'=8,'ja'=4,'ka'=8] {'ja'}, dimensions={1}, use_global_device_ids=true | all-gather | bytes 983040 | tf_op jit(solution)/shard_map/all_gather | solution.py:24
  19.2 184.6 %all-gather.5.cloned.1.call-done = bf16[768,6144]{1,0:T(8,128)(2,1)} async-done(((bf16[96,6144]{1,0:T(8,128)(2,1)}), bf16[768,6144]{1,0:T(8,128)(2,1)}) %all-gather.5.cloned.1.call-update) | async-done | bytes 9437200 | tf_op jit(solution)/shard_map/all_gather | solution.py:25
  203.8 10.7 %convolution_convert_fusion.1 = bf16[512,6144]{1,0:T(8,128)(2,1)} fusion(bf16[512,768]{0,1:T(8,128)(2,1)S(1)} %all_gather.11, bf16[768,6144]{1,0:T(8,128)(2,1)} %all-gather.5.cloned.1.call-done), kind=kOutput, calls=%fused_computation.12 | convolution fusion | flops 4834983936 | bytes 16515072 | tf_op jit(solution)/shard_map/dot_general | solution.py:29
  214.5 0.0 reduce-scatter.8.cloned.1.call-update
  214.6 0.0 reduce-scatter.6.cloned.1.call-start
  214.6 66.5 %all-gather.3.cloned.1.call-done = bf16[512,6144]{1,0:T(8,128)(2,1)} async-done(((bf16[512,768]{1,0:T(8,128)(2,1)}), bf16[512,6144]{1,0:T(8,128)(2,1)}) %all-gather.3.cloned.1.call-update) | async-done | bytes 6291472 | tf_op jit(solution)/shard_map/all_gather | solution.py:22
  281.1 11.0 %convolution_convert_fusion.2 = bf16[512,768]{0,1:T(8,128)(2,1)} fusion(bf16[768,6144]{1,0:T(8,128)(2,1)} %all-gather.5.cloned.1.call-done, bf16[512,6144]{1,0:T(8,128)(2,1)} %all-gather.3.cloned.1.call-done), kind=kOutput, calls=%fused_computation.29 | convolution fusion | flops 4863688704 | bytes 16515072 | tf_op jit(solution)/shard_map/dot_general | solution.py:26
  292.1 0.0 reduce-scatter.6.cloned.1.call-update
  292.1 0.0 reduce-scatter.10.cloned.1.call-start
  292.2 13.1 %fusion.5 = bf16[768,6144]{0,1:T(8,128)(2,1)} fusion(bf16[512,768]{0,1:T(8,128)(2,1)S(1)} %all_gather.11, bf16[512,6144]{1,0:T(8,128)(2,1)} %all-gather.3.cloned.1.call-done), kind=kOutput, calls=%fused_computation.11 | convolution fusion | flops 4868014080 | bytes 16515072 | tf_op jit(solution)/shard_map/dot_general | solution.py:35
  305.3 12.7 %copy.8 = bf16[768,6144]{1,0:T(8,128)(2,1)} copy(bf16[768,6144]{0,1:T(8,128)(2,1)} %fusion.5) | data formatting | bytes 18874368
  318.0 0.0 copy-start
  318.0 0.0 reduce-scatter.10.cloned.1.call-update
  318.0 39.4 %reduce-scatter.8.cloned.1.call-done = bf16[512,768]{1,0:T(8,128)(2,1)} async-done(((bf16[512,6144]{1,0:T(8,128)(2,1)}), bf16[512,768]{1,0:T(8,128)(2,1)}) %reduce-scatter.8.cloned.1.call-update) | async-done | bytes 786448 | tf_op jit(solution)/shard_map/reduce_scatter | solution.py:31
  357.4 0.0 copy-done
  357.4 3.1 fusion.13
  360.5 34.1 %reduce-scatter.6.cloned.1.call-done = bf16[512,192]{0,1:T(8,128)(2,1)} async-done(((bf16[512,768]{0,1:T(8,128)(2,1)}), bf16[512,192]{0,1:T(8,128)(2,1)}) %reduce-scatter.6.cloned.1.call-update) | async-done | bytes 196624 | tf_op jit(solution)/shard_map/reduce_scatter | solution.py:30
  394.6 194.1 %reduce-scatter.10.cloned.1.call-done = bf16[96,6144]{1,0:T(8,128)(2,1)} async-done(((bf16[768,6144]{1,0:T(8,128)(2,1)}), bf16[96,6144]{1,0:T(8,128)(2,1)}) %reduce-scatter.10.cloned.1.call-update) | async-done | bytes 1179664
Async XLA Ops:
  7.2 196.7 %all-gather.5.cloned.1.call-start = ((), (), s32[]{:S(2)}) async-start(), calls=%async_computation.4 | async-start | bytes 10616832 | tf_op jit(solution)/shard_map/all_gather | solution.py:25
  7.9 273.2 %all-gather.3.cloned.1.call-start = ((), (), s32[]{:S(2)}) async-start(), calls=%async_computation.3 | async-start | bytes 7077888 | tf_op jit(solution)/shard_map/all_gather | solution.py:22
  8.6 348.8 %reduce-scatter.8.cloned.1.call-start = ((), (), s32[]{:S(2)}) async-start(), calls=%async_computation.6 | async-start | bytes 7077888 | tf_op jit(solution)/shard_map/reduce_scatter | solution.py:31
  214.6 180.1 %reduce-scatter.6.cloned.1.call-start = ((), (), s32[]{:S(2)}) async-start(), calls=%async_computation.5 | async-start | bytes 983040 | tf_op jit(solution)/shard_map/reduce_scatter | solution.py:30
  292.1 296.5 %reduce-scatter.10.cloned.1.call-start = ((), (), s32[]{:S(2)}) async-start(), calls=%async_computation.7 | async-start | bytes 10616832
  318.0 39.4 %copy-start = (bf16[512,768]{1,0:T(8,128)(2,1)S(1)}, bf16[512,768]{1,0:T(8,128)(2,1)}, u32[]{:S(2)}) copy-start(bf16[512,768]{1,0:T(8,128)(2,1)} %param.3) | copy-start | bytes 2359300
Sparse Core Ops, SparseCore 0:
  9.8 194.0 all-gather.4
  205.6 75.4 all-gather.2
  283.7 73.6 reduce-scatter.7
  360.6 33.9 reduce-scatter.5
  397.8 190.8 reduce-scatter.9
where the time goes:
time: 597 us; the launch traced here: 595 us
  waiting for transfers between devices  520 us (87%)
  matrix products  34.8 us (6%)
  between operations  13.8 us (2%)
  local copies, waits for them, and re-layouts  12.7 us (2%)
  blocking collectives  10.5 us (2%)
    unnamed x6, waiting for transfers between devices  195 us
    all_gather x1, waiting for transfers between devices, shards(): weight_block = lax.all_gather(down_weight, 'ia', axis=0, tiled=True)  185 us
    all_gather x1, waiting for transfers between devices, shards(): pre_block = lax.all_gather(pre_act, 'ka', axis=1, tiled=True)  66.5 us
    reduce_scatter x1, waiting for transfers between devices, shards(): lax.psum_scatter(hidden_terms.astype(jnp.bfloat16), 'ka', scatter_dimensi...  39.4 us
    reduce_scatter x1, waiting for transfers between devices, shards(): lax.psum_scatter(out_terms.astype(jnp.bfloat16), 'ja', scatter_dimension=...  34.1 us
    dot_general x1, matrix products, shards(): lax.dot_general(grad_block, hidden, (((0,), (0,)), ((), ())), preferred_e...  13.1 us
    unnamed x3, local copies, waits for them, and re-layouts  12.7 us
  transfers between devices with their start and end apart: 5, of which 5 were waited for; matrix products, arithmetic and copies ran while one was open for 9% of the time, Pallas kernels for 0%

commit v1 on v0

v1 whole, which is shorter than its diff:
```python
import jax
import jax.numpy as jnp
from jax import lax
from jax.experimental import pallas as pl
from jax.experimental.pallas import tpu as pltpu
from jax.sharding import Mesh
from jax.sharding import PartitionSpec as P

coeff = 0.7978845608028654
bf16 = jnp.bfloat16
f32 = jnp.float32


def gelu_value(v):
    return 0.5 * v * (1.0 + jnp.tanh(coeff * (v + 0.044715 * v * v * v)))


def gelu_slope(v):
    tval = jnp.tanh(coeff * (v + 0.044715 * v * v * v))
    return 0.5 * (1.0 + tval) + 0.5 * v * (1.0 - tval * tval) * coeff * (
        1.0 + 3.0 * 0.044715 * v * v
    )


def swap_y(a, mask):
    flip = (mask & 1) * 2 + (mask >> 1)
    return lax.ppermute(a, ("yl", "yh"), [(i, i ^ flip) for i in range(4)])


def swap_x(a, mask):
    return lax.ppermute(a, "x", [(i, i ^ mask) for i in range(4)])


def swap_c(a):
    return lax.ppermute(a, "c", [(0, 1), (1, 0)])


def near4(swap, own):
    return swap(own, 1), swap(own, 3)


def far4(swap, near1, near3):
    half = near1.shape[0] // 2
    return swap(near1[:half], 3), swap(near3[half:], 1)


def add(a, b):
    return (a.astype(f32) + b.astype(f32)).astype(bf16)


def scatter_far(swap, far):
    half = far.shape[0] // 2
    return swap(far[:half], 1), swap(far[half:], 3)


def scatter_near(swap, near1, near3, far1, far3):
    half = far1.shape[0]
    near3 = jnp.concatenate([add(near3[:half], far1), near3[half:]], axis=0)
    near1 = jnp.concatenate([near1[:half], add(near1[half:], far3)], axis=0)
    return swap(near1, 1), swap(near3, 3)


def add3(own, got1, got3):
    return own.astype(f32) + got1.astype(f32) + got3.astype(f32)


def after(value, *others):
    return lax.optimization_barrier((value,) + others)[0]


def split_kernel(which_ref, a_ref, mine_ref, theirs_ref):
    which = which_ref[0]
    for value, low_ref, high_ref in ((0, mine_ref, theirs_ref), (1, theirs_ref, mine_ref)):

        @pl.when(which == value)
        def _(low_ref=low_ref, high_ref=high_ref):
            for k in range(a_ref.shape[1] // 768):
                low_ref[:, 384 * k : 384 * k + 384] = a_ref[:, 768 * k : 768 * k + 384]
                high_ref[:, 384 * k : 384 * k + 384] = a_ref[:, 768 * k + 384 : 768 * k + 768]


def split_columns(a, which):
    half = jax.ShapeDtypeStruct((a.shape[0], a.shape[1] // 2), a.dtype)
    return pl.pallas_call(
        split_kernel,
        out_shape=(half, half),
        in_specs=[pl.BlockSpec(memory_space=pltpu.SMEM), pl.BlockSpec(memory_space=pltpu.VMEM)],
        out_specs=(pl.BlockSpec(memory_space=pltpu.VMEM),) * 2,
        cost_estimate=pl.CostEstimate(flops=0, bytes_accessed=4 * a.size, transcendentals=0),
    )(which.astype(jnp.int32).reshape(1), a)


def join_columns(mine, theirs, which):
    low = jnp.where(which == 0, mine, theirs)
    high = jnp.where(which == 0, theirs, mine)
    n = mine.shape[1] // 384
    return jnp.concatenate([p[:, 384 * k : 384 * k + 384] for k in range(n) for p in (low, high)], axis=1)


def shards(pre_act, down_weight, grad_out):
    x, yl, yh, c = (lax.axis_index(n) for n in ("x", "yl", "yh", "c"))
    pre32 = pre_act.astype(f32)
    hid = gelu_value(pre32).astype(bf16)
    low, high = hid[:, :384], hid[:, 384:]
    keep, give = jnp.where(yl == 0, low, high), jnp.where(yl == 0, high, low)
    hidden = [lax.all_gather(keep, "z", axis=1, tiled=True)]
    got_h = swap_y(give, 1)
    hidden.append(lax.all_gather(got_h, "z", axis=1, tiled=True))

    keep, give = split_columns(down_weight, yl)
    own = jnp.concatenate([keep, swap_y(give, 1)], axis=0)
    near = near4(swap_x, own)
    weight = jnp.concatenate([own, near[0], *far4(swap_x, *near), near[1]], axis=0)

    small = grad_out.T
    got = [small] + [swap_y(small, m) for m in (1, 2, 3)]
    part = jnp.stack([jnp.concatenate([got[2 * h], got[2 * h + 1]], axis=1) for h in range(2)])
    table = jnp.concatenate([part, swap_c(part)], axis=0).reshape(8, 96, 1024)
    flip = x ^ (yh * 2 + c)
    iota = jnp.arange(8, dtype=jnp.int32)
    place = flip ^ (iota >> 1)
    grads = table[(place & 1) * 4 + (place >> 1) * 2 + (yl ^ (iota & 1))].reshape(768, 1024)
    grads = [grads[:, :512], grads[:, 512:]]

    gh = []
    for t in (1, 0):
        part = lax.dot_general(weight, grads[t], (((0,), (0,)), ((), ())), preferred_element_type=f32).astype(bf16)
        part = after(part, hidden[1], *gh)
        gh.append(lax.psum_scatter(part, "z", scatter_dimension=0, tiled=True))
    mine, theirs = gh[1].T, swap_y(gh[0], 1).T
    grad_hidden = join_columns(mine, theirs, yl)
    grad_pre = (grad_hidden.astype(f32) * gelu_slope(pre32)).astype(bf16)

    gw = sum(jnp.dot(grads[t], hidden[t], preferred_element_type=f32) for t in range(2))
    gw = gw.astype(bf16).reshape(4, 192, 3072)
    sent = scatter_far(swap_x, gw[2])
    total = add3(gw[0], *scatter_near(swap_x, gw[1], gw[3], *sent)).astype(bf16)
    grad_weight = join_columns(total[:96], swap_y(total[96:], 1), yl)

    order = (flip ^ (((iota >> 1) & 1) * 2 + (iota >> 2))) * 2 + ((iota & 1) ^ yl)
    total = jnp.zeros((192, 512), f32)
    for t in (1, 0):
        out = lax.dot_general(weight, after(hidden[t], gw), (((1,), (1,)), ((), ())), preferred_element_type=f32)
        out = out.astype(bf16).reshape(8, 96, 512)
        part = add(out[order[:4]], swap_c(out[order[4:]])).reshape(2, 192, 512)
        for h in (1, 0):
            total = total + (swap_y(part[h], 2 * h + t) if h + t else part[h]).astype(f32)
    output = total.astype(bf16).T
    return output, grad_pre, grad_weight


def solution(mesh):
    cube = Mesh(mesh.devices.reshape(4, 2, 2, 2, 8), ("x", "yl", "yh", "c", "z"))
    t, f, d = ("x", "yl"), ("yh", "c", "z"), ("z", "x", "yl")
    e = ("z", "yh", "c")
    return jax.shard_map(
        shards,
        mesh=cube,
        in_specs=(P(t, f), P(d, ("yh", "c")), P(t, e)),
        out_specs=(P(t, e), P(t, f), P(d, ("yh", "c"))),
        check_vma=False,
    )
```

time: 597 us -> 222 us (0.37)
  waiting for transfers between devices: 520 us -> 104 us
  starting transfers between devices: 0.2 us -> 29 us
  local copies, waits for them, and re-layouts: 12.7 us -> 25.8 us
  other arithmetic: 3.11 us -> 14.8 us
  blocking collectives: 10.5 us -> 0 us
    all_gather x2, waiting for transfers between devices: 251 us -> 10 us  [the longest x1 10 us: shards(): hidden = [lax.all_gather(keep, 'z', axis=1, tiled=True)]]
    unnamed x6 -> x4, waiting for transfers between devices: 195 us -> 0.75 us
    ppermute x0 -> x21, waiting for transfers between devices: none -> 80.9 us  [the longest x10 47.2 us: swap_y(): return lax.ppermute(a, ('yl', 'yh'), [(i, i ^ flip) for i in range(4)])]
    reduce_scatter x2, waiting for transfers between devices: 73.5 us -> 12.1 us  [shards(): gh.append(lax.psum_scatter(part, 'z', scatter_dimension=0, tiled=True))]
    ppermute x0 -> x21, starting transfers between devices: none -> 28.7 us  [the longest x10 15.5 us: swap_y(): return lax.ppermute(a, ('yl', 'yh'), [(i, i ^ flip) for i in range(4)])]
    all_gather x1 -> x0, blocking collectives: 10.5 us -> none  [shards(): grad_block = lax.all_gather(grad_out, 'ja', axis=1, tiled=True)]
    gather x0 -> x5, local copies, waits for them, and re-layouts: none -> 7.14 us  [the longest x4 5.34 us: shards(): part = add(out[order[:4]], swap_c(out[order[4:]])).reshape(2, 192, 512)]
    dot_general x3 -> x6, matrix products: 34.8 us -> 31.6 us  [the longest x2 13.1 us: shards(): lax.dot_general(weight, grads[t], (((0,), (0,)), ((), ())), preferred_ele...]
  transfers between devices with their start and end apart: 5 -> 25, of which waited for: 5 -> 17; matrix products, arithmetic and copies ran while one was open for 9% -> 29% of each run, Pallas kernels for 0% -> 1%
where the time goes in v1:
time: 222 us; the launch traced here: 221 us
  waiting for transfers between devices  104 us (47%)
  matrix products  31.6 us (14%)
  starting transfers between devices  29 us (13%)
  local copies, waits for them, and re-layouts  25.8 us (12%)
  other arithmetic  14.8 us (7%)
  between operations  14.1 us (6%)
  Pallas kernels  2.4 us (1%)
    ppermute x10, waiting for transfers between devices, swap_y(): return lax.ppermute(a, ('yl', 'yh'), [(i, i ^ flip) for i in range(4)])  47.2 us
    ppermute x8, waiting for transfers between devices, swap_x(): return lax.ppermute(a, 'x', [(i, i ^ mask) for i in range(4)])  33.8 us
    ppermute x10, starting transfers between devices, swap_y(): return lax.ppermute(a, ('yl', 'yh'), [(i, i ^ flip) for i in range(4)])  15.5 us
    dot_general x2, matrix products, shards(): lax.dot_general(weight, grads[t], (((0,), (0,)), ((), ())), preferred_ele...  13.1 us
    ppermute x8, starting transfers between devices, swap_x(): return lax.ppermute(a, 'x', [(i, i ^ mask) for i in range(4)])  12.9 us
    reduce_scatter x2, waiting for transfers between devices, shards(): gh.append(lax.psum_scatter(part, 'z', scatter_dimension=0, tiled=True))  12.1 us
    unnamed x41, local copies, waits for them, and re-layouts  11.5 us
    dot_general x2, matrix products, shards(): lax.dot_general(weight, after(hidden[t], gw), (((1,), (1,)), ((), ())), p...  10.8 us
  transfers between devices with their start and end apart: 25, of which 17 were waited for; matrix products, arithmetic and copies ran while one was open for 29% of the time, Pallas kernels for 1%

profile of v1, /device:TPU:2, one launch (start us, length us, event | category | flops | bytes accessed | tf_op | source)
XLA Modules:
  0.0 221.5 jit_solution(13342092677207557858)
XLA Ops:
  7.2 1.4 copy.6
  9.2 0.8 broadcast_select_fusion.3
  10.0 1.6 collective-permute-start.5
  11.6 9.3 %collective-permute-done.5 = bf16[512,384]{0,1:T(8,128)(2,1)S(1)} collective-permute-done((bf16[512,384]{0,1:T(8,128)(2,1)S(1)}, bf16[512,384]{0,1:T(8,128)(2,1)S(1)}, u32[]{:S(2)}, u32[]{:S(2)}) %collective-permute-start.5) | collective-permute-done | bytes 393248 | tf_op jit(solution)/shard_map/ppermute | solution.py:27
  22.4 2.4 %shard_map.58 = (bf16[96,3072]{1,0:T(8,128)(2,1)}, bf16[96,3072]{1,0:T(8,128)(2,1)}) custom-call(s32[1]{0:T(128)} %bitcast.which_ref, bf16[96,6144]{1,0:T(8,128)(2,1)} %a_ref.1), custom_call_target="tpu_custom_call" | custom-call | bytes 2359296 | tf_op jit(solution)/shard_map/pallas_call | solution.py:84
  24.8 1.6 collective-permute-start
  26.8 2.2 %constant_dynamic-update-slice_fusion.1 = (bf16[192,3072]{1,0:T(8,128)(2,1)}, bf16[768,3072]{1,0:T(8,128)(2,1)}) fusion(bf16[96,3072]{1,0:T(8,128)(2,1)} %get-tuple-element.9), kind=kLoop, calls=%fused_computation.70 | loop fusion | bytes 1769472
  29.1 12.2 %collective-permute-done = bf16[96,3072]{1,0:T(8,128)(2,1)S(1)} collective-permute-done((bf16[96,3072]{1,0:T(8,128)(2,1)}, bf16[96,3072]{1,0:T(8,128)(2,1)S(1)}, u32[]{:S(2)}, u32[]{:S(2)}) %collective-permute-start) | collective-permute-done | bytes 589856 | tf_op jit(solution)/shard_map/ppermute | solution.py:27
  41.3 1.2 constant_dynamic-update-slice_fusion
  42.7 3.5 %collective-permute-start.7 = (bf16[192,512]{1,0:T(8,128)(2,1)S(1)}, bf16[192,512]{1,0:T(8,128)(2,1)S(1)}, u32[]{:S(2)}, u32[]{:S(2)}) collective-permute-start(bf16[192,512]{1,0:T(8,128)(2,1)S(1)} %bitcast.41), channel_id=1, source_target_pairs={{0,16},{16,0},{32,48},{48,32},{1,17},{17,1},{33,49},{49,33},{2,18}... | collective-permute-start | bytes 589832 | tf_op jit(solution)/shard_map/ppermute | solution.py:27
  46.2 0.9 collective-permute-start.8
  47.1 2.4 %collective-permute-start.3 = (bf16[192,3072]{1,0:T(8,128)(2,1)}, bf16[192,3072]{1,0:T(8,128)(2,1)}, u32[]{:S(2)}, u32[]{:S(2)}) collective-permute-start(bf16[192,3072]{1,0:T(8,128)(2,1)} %get-tuple-element.30), channel_id=1, source_target_pairs={{0,192},{64,128},{128,64},{192,0},{1,193},{65,129},{129,65},{193,1... | collective-permute-start | bytes 3538952 | tf_op jit(solution)/shard_map/ppermute | solution.py:31
  50.2 2.9 %collective-permute-done.8 = bf16[192,512]{1,0:T(8,128)(2,1)S(1)} collective-permute-done((bf16[192,512]{1,0:T(8,128)(2,1)S(1)}, bf16[192,512]{1,0:T(8,128)(2,1)S(1)}, u32[]{:S(2)}, u32[]{:S(2)}) %collective-permute-start.8) | collective-permute-done | bytes 196640 | tf_op jit(solution)/shard_map/ppermute | solution.py:27
  53.1 1.0 pad_maximum_fusion.3
  54.1 12.4 %collective-permute-done.1 = bf16[192,3072]{1,0:T(8,128)(2,1)S(1)} collective-permute-done((bf16[192,3072]{1,0:T(8,128)(2,1)}, bf16[192,3072]{1,0:T(8,128)(2,1)S(1)}, u32[]{:S(2)}, u32[]{:S(2)}) %collective-permute-start.1) | collective-permute-done | bytes 1179680 | tf_op jit(solution)/shard_map/ppermute | solution.py:31
  66.5 0.9 slice.180
  67.5 1.5 collective-permute-start.2
  69.0 1.3 pad_maximum_fusion
  70.3 1.8 gather_fusion
  72.1 4.6 %collective-permute-done.3 = bf16[192,3072]{1,0:T(8,128)(2,1)} collective-permute-done((bf16[192,3072]{1,0:T(8,128)(2,1)}, bf16[192,3072]{1,0:T(8,128)(2,1)}, u32[]{:S(2)}, u32[]{:S(2)}) %collective-permute-start.3) | collective-permute-done | bytes 1179680 | tf_op jit(solution)/shard_map/ppermute | solution.py:31
  76.6 1.1 slice.181
  77.7 2.8 %collective-permute-start.4 = (bf16[96,3072]{1,0:T(8,128)(2,1)S(1)}, bf16[96,3072]{1,0:T(8,128)(2,1)S(1)}, u32[]{:S(2)}, u32[]{:S(2)}) collective-permute-start(bf16[96,3072]{1,0:T(8,128)(2,1)S(1)} %slice.181), channel_id=1, source_target_pairs={{0,64},{64,0},{128,192},{192,128},{1,65},{65,1},{129,193},{193,129... | collective-permute-start | bytes 1769480 | tf_op jit(solution)/shard_map/ppermute | solution.py:31
  80.5 1.1 constant_dynamic-update-slice_fusion.5
  81.6 2.1 collective-permute-done.2
  83.7 2.0 constant_dynamic-update-slice_fusion.4
  85.7 2.6 %collective-permute-done.4 = bf16[96,3072]{1,0:T(8,128)(2,1)S(1)} collective-permute-done((bf16[96,3072]{1,0:T(8,128)(2,1)S(1)}, bf16[96,3072]{1,0:T(8,128)(2,1)S(1)}, u32[]{:S(2)}, u32[]{:S(2)}) %collective-permute-start.4) | collective-permute-done | bytes 589856 | tf_op jit(solution)/shard_map/ppermute | solution.py:31
  88.3 0.9 constant_dynamic-update-slice_fusion.3
  89.3 2.4 %constant_dynamic-update-slice_fusion.2 = bf16[768,3072]{1,0:T(8,128)(2,1)} fusion(bf16[768,3072]{1,0:T(8,128)(2,1)} %constant_dynamic-update-slice_fusion.3, bf16[192,3072]{1,0:T(8,128)(2,1)} %collective-permute-done.3), kind=kLoop, calls=%fused_computation.71 | loop fusion | bytes 2359296 | tf_op jit(solution)/shard_map/concatenate | solution.py:113
  91.6 6.6 %convolution_convert_fusion = bf16[3072,512]{1,0:T(8,128)(2,1)} fusion(bf16[768,3072]{1,0:T(8,128)(2,1)} %constant_dynamic-update-slice_fusion.2, bf16[768,1024]{1,0:T(8,128)(2,1)S(1)} %bitcast.34), kind=kOutput, calls=%fused_computation.6 | convolution fusion | flops 2417491968 | bytes 8650752 | tf_op jit(solution)/shard_map/dot_general | solution.py:127
  98.6 6.6 %convolution_convert_fusion.1 = bf16[3072,512]{1,0:T(8,128)(2,1)} fusion(bf16[768,3072]{1,0:T(8,128)(2,1)} %constant_dynamic-update-slice_fusion.2, bf16[768,1024]{1,0:T(8,128)(2,1)S(1)} %bitcast.35), kind=kOutput, calls=%fused_computation.7 | convolution fusion | flops 2417491968 | bytes 8650752 | tf_op jit(solution)/shard_map/dot_general | solution.py:127
  105.1 10.0 %all-gather.5.cloned.1.call-done = bf16[512,3072]{0,1:T(8,128)(2,1)} async-done(((bf16[512,384]{0,1:T(8,128)(2,1)}), bf16[512,3072]{0,1:T(8,128)(2,1)}) %all-gather.5.cloned.1.call-update) | async-done | bytes 3145744 | tf_op jit(solution)/shard_map/all_gather | solution.py:106
  115.2 4.7 %fusion.14 = f32[768,3072]{1,0:T(8,128)S(1)} fusion(bf16[512,3072]{0,1:T(8,128)(2,1)} %all-gather.5.cloned.1.call-done, bf16[768,1024]{1,0:T(8,128)(2,1)S(1)} %bitcast.36), kind=kOutput, calls=%fused_computation.40 | convolution fusion | flops 2415919104 | bytes 13369344 | tf_op jit(solution)/shard_map/dot_general | solution.py:134
  119.8 2.9 %add_convert_fusion = bf16[768,3072]{1,0:T(8,128)(2,1)S(1)} fusion(f32[768,3072]{1,0:T(8,128)S(1)} %fusion.14, bf16[512,3072]{0,1:T(8,128)(2,1)S(1)} %copy-done.2, bf16[768,1024]{1,0:T(8,128)(2,1)S(1)} %bitcast.37), kind=kOutput, calls=%fused_computation.5 | convolution fusion | flops 2420637696 | bytes 18087936 | tf_op jit(solution)/shard_map/dot_general | solution.py:134
  122.8 1.4 fusion.25
  124.2 1.1 copy-done
  125.3 1.5 collective-permute-start.16
  126.8 1.8 collective-permute-start.18
  128.6 4.9 %convolution_convert_fusion.3 = bf16[768,512]{1,0:T(8,128)(2,1)S(1)} fusion(bf16[768,3072]{1,0:T(8,128)(2,1)} %constant_dynamic-update-slice_fusion.2, bf16[512,3072]{0,1:T(8,128)(2,1)S(1)} %copy-done.2), kind=kOutput, calls=%fused_computation.29 | convolution fusion | flops 2416312320 | bytes 8650752 | tf_op jit(solution)/shard_map/dot_general | solution.py:143
  133.5 1.3 gather_fusion.2
  135.5 5.0 %collective-permute-done.16 = bf16[96,3072]{1,0:T(8,128)(2,1)} collective-permute-done((bf16[96,3072]{1,0:T(8,128)(2,1)}, bf16[96,3072]{1,0:T(8,128)(2,1)}, u32[]{:S(2)}, u32[]{:S(2)}) %collective-permute-start.16) | collective-permute-done | bytes 589856 | tf_op jit(solution)/shard_map/ppermute | solution.py:31
  140.5 1.2 collective-permute-done.18
  141.7 2.0 add_convert_fusion.3
  143.9 1.8 collective-permute-start.17
  145.7 1.1 pad_maximum_fusion.2
  146.8 0.9 collective-permute-start.19
  147.7 5.9 %convolution_convert_fusion.2 = bf16[768,512]{1,0:T(8,128)(2,1)} fusion(bf16[768,3072]{1,0:T(8,128)(2,1)} %constant_dynamic-update-slice_fusion.2, bf16[512,3072]{0,1:T(8,128)(2,1)S(1)} %copy-done.8), kind=kOutput, calls=%fused_computation.28 | convolution fusion | flops 2416312320 | bytes 8650752 | tf_op jit(solution)/shard_map/dot_general | solution.py:143
  153.6 1.7 gather_fusion.4
  155.3 1.7 gather_fusion.3
  157.3 1.1 add_convert_fusion.5
  158.4 4.7 %reduce-scatter.3.cloned.1.call-done = bf16[384,512]{1,0:T(8,128)(2,1)} async-done(((bf16[3072,512]{1,0:T(8,128)(2,1)}), bf16[384,512]{1,0:T(8,128)(2,1)}) %reduce-scatter.3.cloned.1.call-update) | async-done | bytes 393232 | tf_op jit(solution)/shard_map/reduce_scatter | solution.py:129
  163.2 2.8 %collective-permute-start.11 = (bf16[192,512]{1,0:T(8,128)(2,1)S(1)}, bf16[192,512]{1,0:T(8,128)(2,1)S(1)}, u32[]{:S(2)}, u32[]{:S(2)}) collective-permute-start(bf16[192,512]{1,0:T(8,128)(2,1)S(1)} %bitcast.45), channel_id=1, source_target_pairs={{0,48},{16,32},{32,16},{48,0},{1,49},{17,33},{33,17},{49,1},{2,50}... | collective-permute-start | bytes 589832 | tf_op jit(solution)/shard_map/ppermute | solution.py:27
  166.3 1.1 add_convert_fusion.4
  167.4 3.0 %collective-permute-done.17 = bf16[192,3072]{1,0:T(8,128)(2,1)} collective-permute-done((bf16[192,3072]{1,0:T(8,128)(2,1)S(1)}, bf16[192,3072]{1,0:T(8,128)(2,1)}, u32[]{:S(2)}, u32[]{:S(2)}) %collective-permute-start.17) | collective-permute-done | bytes 1179680 | tf_op jit(solution)/shard_map/ppermute | solution.py:31
  170.4 2.7 %collective-permute-done.19 = bf16[192,3072]{1,0:T(8,128)(2,1)} collective-permute-done((bf16[192,3072]{1,0:T(8,128)(2,1)}, bf16[192,3072]{1,0:T(8,128)(2,1)}, u32[]{:S(2)}, u32[]{:S(2)}) %collective-permute-start.19) | collective-permute-done | bytes 1179680 | tf_op jit(solution)/shard_map/ppermute | solution.py:31
  173.1 2.6 %add_convert_fusion.1 = bf16[192,3072]{1,0:T(8,128)(2,1)S(1)} fusion(bf16[192,3072]{1,0:T(8,128)(2,1)} %collective-permute-done.19, bf16[192,3072]{1,0:T(8,128)(2,1)} %collective-permute-done.17, bf16[768,3072]{1,0:T(8,128)(2,1)} %copy-done), kind=kLoop, calls=%fused_computation.15 | loop fusion | flops 3538944 | bytes 4718592 | tf_op jit(solution)/shard_map/convert_element_type | solution.py:137
  175.7 1.5 collective-permute-start.20
  177.3 2.8 %collective-permute-start.14 = (bf16[192,512]{1,0:T(8,128)(2,1)S(1)}, bf16[192,512]{1,0:T(8,128)(2,1)S(1)}, u32[]{:S(2)}, u32[]{:S(2)}) collective-permute-start(bf16[192,512]{1,0:T(8,128)(2,1)S(1)} %bitcast.46), channel_id=1, source_target_pairs={{0,16},{16,0},{32,48},{48,32},{1,17},{17,1},{33,49},{49,33},{2,18}... | collective-permute-start | bytes 589832 | tf_op jit(solution)/shard_map/ppermute | solution.py:27
  180.1 14.5 %collective-permute-done.14 = bf16[192,512]{1,0:T(8,128)(2,1)S(1)} collective-permute-done((bf16[192,512]{1,0:T(8,128)(2,1)S(1)}, bf16[192,512]{1,0:T(8,128)(2,1)S(1)}, u32[]{:S(2)}, u32[]{:S(2)}) %collective-permute-start.14) | collective-permute-done | bytes 196640 | tf_op jit(solution)/shard_map/ppermute | solution.py:27
  194.6 0.8 fusion.17
  196.6 7.6 %collective-permute-done.15 = bf16[384,512]{1,0:T(8,128)(2,1)S(1)} collective-permute-done((bf16[384,512]{1,0:T(8,128)(2,1)S(1)}, bf16[384,512]{1,0:T(8,128)(2,1)S(1)}, u32[]{:S(2)}, u32[]{:S(2)}) %collective-permute-start.15) | collective-permute-done | bytes 393248 | tf_op jit(solution)/shard_map/ppermute | solution.py:27
  204.3 7.4 %reduce-scatter.5.cloned.1.call-done = bf16[384,512]{1,0:T(8,128)(2,1)} async-done(((bf16[3072,512]{1,0:T(8,128)(2,1)}), bf16[384,512]{1,0:T(8,128)(2,1)}) %reduce-scatter.5.cloned.1.call-update) | async-done | bytes 393232 | tf_op jit(solution)/shard_map/reduce_scatter | solution.py:129
  211.6 1.1 select_bitcast_fusion.1
  212.7 1.1 fusion.7
  213.8 1.2 copy.7
  (74 shorter events, 6.4 us)
Async XLA Ops:
  7.2 91.1 %all-gather.3.cloned.1.call-start = ((), (), s32[]{:S(2)}) async-start(), calls=%async_computation.2 | async-start | bytes 3538944 | tf_op jit(solution)/shard_map/all_gather | solution.py:108
  9.2 17.2 %copy-start.6 = (bf16[512,192]{0,1:T(8,128)(2,1)S(1)}, bf16[512,192]{0,1:T(8,128)(2,1)}, u32[]{:S(2)}) copy-start(bf16[512,192]{0,1:T(8,128)(2,1)} %param.5) | copy-start | bytes 589828
  10.0 10.9 %collective-permute-start.5 = (bf16[512,384]{0,1:T(8,128)(2,1)S(1)}, bf16[512,384]{0,1:T(8,128)(2,1)S(1)}, u32[]{:S(2)}, u32[]{:S(2)}) collective-permute-start(bf16[512,384]{0,1:T(8,128)(2,1)S(1)} %get-tuple-element.28), channel_id=1, source_target_pairs={{0,32},{16,48},{32,0},{48,16},{1,33},{17,49},{33,1},{49,17},{2,34}... | collective-permute-start | bytes 1179656 | tf_op jit(solution)/shard_map/ppermute | solution.py:27
  20.9 0.7 copy-start.5
  21.6 93.5 %all-gather.5.cloned.1.call-start = ((), (), s32[]{:S(2)}) async-start(), calls=%async_computation.3 | async-start | bytes 3538944 | tf_op jit(solution)/shard_map/all_gather | solution.py:106
  22.4 140.8 %reduce-scatter.3.cloned.1.call-start = ((), (), s32[]{:S(2)}) async-start(), calls=%async_computation.4 | async-start | bytes 3538944 | tf_op jit(solution)/shard_map/reduce_scatter | solution.py:129
  24.8 16.5 %collective-permute-start = (bf16[96,3072]{1,0:T(8,128)(2,1)}, bf16[96,3072]{1,0:T(8,128)(2,1)S(1)}, u32[]{:S(2)}, u32[]{:S(2)}) collective-permute-start(bf16[96,3072]{1,0:T(8,128)(2,1)} %get-tuple-element.10), channel_id=1, source_target_pairs={{0,32},{16,48},{32,0},{48,16},{1,33},{17,49},{33,1},{49,17},{2,34}... | collective-permute-start | bytes 1769480 | tf_op jit(solution)/shard_map/ppermute | solution.py:27
  26.4 20.7 %collective-permute-start.6 = (bf16[192,512]{1,0:T(8,128)(2,1)S(1)}, bf16[192,512]{1,0:T(8,128)(2,1)S(1)}, u32[]{:S(2)}, u32[]{:S(2)}) collective-permute-start(bf16[192,512]{1,0:T(8,128)(2,1)S(1)} %bitcast.40), channel_id=1, source_target_pairs={{0,32},{16,48},{32,0},{48,16},{1,33},{17,49},{33,1},{49,17},{2,34}... | collective-permute-start | bytes 589832 | tf_op jit(solution)/shard_map/ppermute | solution.py:27
  42.5 24.1 %collective-permute-start.1 = (bf16[192,3072]{1,0:T(8,128)(2,1)}, bf16[192,3072]{1,0:T(8,128)(2,1)S(1)}, u32[]{:S(2)}, u32[]{:S(2)}) collective-permute-start(bf16[192,3072]{1,0:T(8,128)(2,1)} %get-tuple-element.30), channel_id=1, source_target_pairs={{0,64},{64,0},{128,192},{192,128},{1,65},{65,1},{129,193},{193,129... | collective-permute-start | bytes 3538952 | tf_op jit(solution)/shard_map/ppermute | solution.py:31
  42.7 7.5 %collective-permute-start.7 = (bf16[192,512]{1,0:T(8,128)(2,1)S(1)}, bf16[192,512]{1,0:T(8,128)(2,1)S(1)}, u32[]{:S(2)}, u32[]{:S(2)}) collective-permute-start(bf16[192,512]{1,0:T(8,128)(2,1)S(1)} %bitcast.41), channel_id=1, source_target_pairs={{0,16},{16,0},{32,48},{48,32},{1,17},{17,1},{33,49},{49,33},{2,18}... | collective-permute-start | bytes 589832 | tf_op jit(solution)/shard_map/ppermute | solution.py:27
  46.2 6.9 %collective-permute-start.8 = (bf16[192,512]{1,0:T(8,128)(2,1)S(1)}, bf16[192,512]{1,0:T(8,128)(2,1)S(1)}, u32[]{:S(2)}, u32[]{:S(2)}) collective-permute-start(bf16[192,512]{1,0:T(8,128)(2,1)S(1)} %bitcast.42), channel_id=1, source_target_pairs={{0,48},{16,32},{32,16},{48,0},{1,49},{17,33},{33,17},{49,1},{2,50}... | collective-permute-start | bytes 589832 | tf_op jit(solution)/shard_map/ppermute | solution.py:27
  47.1 29.5 %collective-permute-start.3 = (bf16[192,3072]{1,0:T(8,128)(2,1)}, bf16[192,3072]{1,0:T(8,128)(2,1)}, u32[]{:S(2)}, u32[]{:S(2)}) collective-permute-start(bf16[192,3072]{1,0:T(8,128)(2,1)} %get-tuple-element.30), channel_id=1, source_target_pairs={{0,192},{64,128},{128,64},{192,0},{1,193},{65,129},{129,65},{193,1... | collective-permute-start | bytes 3538952 | tf_op jit(solution)/shard_map/ppermute | solution.py:31
  54.1 14.9 %collective-permute-start.9 = (bf16[2,192,1024]{2,1,0:T(8,128)(2,1)}, bf16[2,192,1024]{2,1,0:T(8,128)(2,1)}, u32[]{:S(2)}, u32[]{:S(2)}) collective-permute-start(bf16[2,192,1024]{2,1,0:T(8,128)(2,1)} %pad_maximum_fusion.3), channel_id=1, source_target_pairs={{0,8},{8,0},{1,9},{9,1},{2,10},{10,2},{3,11},{11,3},{4,12},{12,4},... | collective-permute-start | bytes 2359304 | tf_op jit(solution)/shard_map/ppermute | solution.py:35
  66.5 2.5 %copy-start.3 = (bf16[192,3072]{1,0:T(8,128)(2,1)}, bf16[192,3072]{1,0:T(8,128)(2,1)S(1)}, u32[]{:S(2)}) copy-start(bf16[192,3072]{1,0:T(8,128)(2,1)S(1)} %collective-permute-done.1) | copy-start | bytes 3538948
  67.5 16.3 %collective-permute-start.2 = (bf16[96,3072]{1,0:T(8,128)(2,1)}, bf16[96,3072]{1,0:T(8,128)(2,1)}, u32[]{:S(2)}, u32[]{:S(2)}) collective-permute-start(bf16[96,3072]{1,0:T(8,128)(2,1)} %slice.180), channel_id=1, source_target_pairs={{0,192},{64,128},{128,64},{192,0},{1,193},{65,129},{129,65},{193,1... | collective-permute-start | bytes 1769480 | tf_op jit(solution)/shard_map/ppermute | solution.py:31
  70.3 10.3 %copy-start.4 = (bf16[192,3072]{1,0:T(8,128)(2,1)S(1)}, bf16[192,3072]{1,0:T(8,128)(2,1)}, u32[]{:S(2)}) copy-start(bf16[192,3072]{1,0:T(8,128)(2,1)} %copy-done.3) | copy-start | bytes 3538948
  77.7 10.6 %collective-permute-start.4 = (bf16[96,3072]{1,0:T(8,128)(2,1)S(1)}, bf16[96,3072]{1,0:T(8,128)(2,1)S(1)}, u32[]{:S(2)}, u32[]{:S(2)}) collective-permute-start(bf16[96,3072]{1,0:T(8,128)(2,1)S(1)} %slice.181), channel_id=1, source_target_pairs={{0,64},{64,0},{128,192},{192,128},{1,65},{65,1},{129,193},{193,129... | collective-permute-start | bytes 1769480 | tf_op jit(solution)/shard_map/ppermute | solution.py:31
  85.7 5.9 %copy-start.1 = (bf16[8,96,1024]{2,1,0:T(8,128)(2,1)S(1)}, bf16[8,96,1024]{2,1,0:T(8,128)(2,1)}, u32[]{:S(2)}) copy-start(bf16[8,96,1024]{2,1,0:T(8,128)(2,1)} %gather_fusion) | copy-start | bytes 4718596
  98.2 113.4 %reduce-scatter.5.cloned.1.call-start = ((), (), s32[]{:S(2)}) async-start(), calls=%async_computation.5 | async-start | bytes 3538944 | tf_op jit(solution)/shard_map/reduce_scatter | solution.py:129
  115.2 4.7 %copy-start.2 = (bf16[512,3072]{0,1:T(8,128)(2,1)S(1)}, bf16[512,3072]{0,1:T(8,128)(2,1)}, u32[]{:S(2)}) copy-start(bf16[512,3072]{0,1:T(8,128)(2,1)} %all-gather.3.cloned.1.call-done) | copy-start | bytes 9437188
  122.8 2.5 %copy-start = (bf16[768,3072]{1,0:T(8,128)(2,1)}, bf16[768,3072]{1,0:T(8,128)(2,1)S(1)}, u32[]{:S(2)}) copy-start(bf16[768,3072]{1,0:T(8,128)(2,1)S(1)} %add_convert_fusion) | copy-start | bytes 14155780
  125.3 15.2 %collective-permute-start.16 = (bf16[96,3072]{1,0:T(8,128)(2,1)}, bf16[96,3072]{1,0:T(8,128)(2,1)}, u32[]{:S(2)}, u32[]{:S(2)}) collective-permute-start(bf16[96,3072]{1,0:T(8,128)(2,1)} %get-tuple-element.21), channel_id=1, source_target_pairs={{0,192},{64,128},{128,64},{192,0},{1,193},{65,129},{129,65},{193,1... | collective-permute-start | bytes 1769480 | tf_op jit(solution)/shard_map/ppermute | solution.py:31
  126.8 14.9 %collective-permute-start.18 = (bf16[96,3072]{1,0:T(8,128)(2,1)}, bf16[96,3072]{1,0:T(8,128)(2,1)}, u32[]{:S(2)}, u32[]{:S(2)}) collective-permute-start(bf16[96,3072]{1,0:T(8,128)(2,1)} %get-tuple-element.20), channel_id=1, source_target_pairs={{0,64},{64,0},{128,192},{192,128},{1,65},{65,1},{129,193},{193,129... | collective-permute-start | bytes 1769480 | tf_op jit(solution)/shard_map/ppermute | solution.py:31
  134.9 22.5 %collective-permute-start.10 = (bf16[4,96,512]{2,1,0:T(8,128)(2,1)}, bf16[4,96,512]{2,1,0:T(8,128)(2,1)}, u32[]{:S(2)}, u32[]{:S(2)}) collective-permute-start(bf16[4,96,512]{2,1,0:T(8,128)(2,1)} %gather_fusion.2), channel_id=1, source_target_pairs={{0,8},{8,0},{1,9},{9,1},{2,10},{10,2},{3,11},{11,3},{4,12},{12,4},... | collective-permute-start | bytes 1179656 | tf_op jit(solution)/shard_map/ppermute | solution.py:35
  143.8 3.9 %copy-start.8 = (bf16[512,3072]{0,1:T(8,128)(2,1)S(1)}, bf16[512,3072]{0,1:T(8,128)(2,1)}, u32[]{:S(2)}) copy-start(bf16[512,3072]{0,1:T(8,128)(2,1)} %all-gather.5.cloned.1.call-done) | copy-start | bytes 9437188
  143.9 26.5 %collective-permute-start.17 = (bf16[192,3072]{1,0:T(8,128)(2,1)S(1)}, bf16[192,3072]{1,0:T(8,128)(2,1)}, u32[]{:S(2)}, u32[]{:S(2)}) collective-permute-start(bf16[192,3072]{1,0:T(8,128)(2,1)S(1)} %pad_maximum_fusion.1), channel_id=1, source_target_pairs={{0,64},{64,0},{128,192},{192,128},{1,65},{65,1},{129,193},{193,129... | collective-permute-start | bytes 3538952 | tf_op jit(solution)/shard_map/ppermute | solution.py:31
  146.8 26.3 %collective-permute-start.19 = (bf16[192,3072]{1,0:T(8,128)(2,1)}, bf16[192,3072]{1,0:T(8,128)(2,1)}, u32[]{:S(2)}, u32[]{:S(2)}) collective-permute-start(bf16[192,3072]{1,0:T(8,128)(2,1)} %pad_maximum_fusion.2), channel_id=1, source_target_pairs={{0,192},{64,128},{128,64},{192,0},{1,193},{65,129},{129,65},{193,1... | collective-permute-start | bytes 3538952 | tf_op jit(solution)/shard_map/ppermute | solution.py:31
  157.0 9.3 %collective-permute-start.13 = (bf16[4,96,512]{2,1,0:T(8,128)(2,1)S(1)}, bf16[4,96,512]{2,1,0:T(8,128)(2,1)}, u32[]{:S(2)}, u32[]{:S(2)}) collective-permute-start(bf16[4,96,512]{2,1,0:T(8,128)(2,1)S(1)} %gather_fusion.4), channel_id=1, source_target_pairs={{0,8},{8,0},{1,9},{9,1},{2,10},{10,2},{3,11},{11,3},{4,12},{12,4},... | collective-permute-start | bytes 1179656 | tf_op jit(solution)/shard_map/ppermute | solution.py:35
  163.2 16.9 %collective-permute-start.11 = (bf16[192,512]{1,0:T(8,128)(2,1)S(1)}, bf16[192,512]{1,0:T(8,128)(2,1)S(1)}, u32[]{:S(2)}, u32[]{:S(2)}) collective-permute-start(bf16[192,512]{1,0:T(8,128)(2,1)S(1)} %bitcast.45), channel_id=1, source_target_pairs={{0,48},{16,32},{32,16},{48,0},{1,49},{17,33},{33,17},{49,1},{2,50}... | collective-permute-start | bytes 589832 | tf_op jit(solution)/shard_map/ppermute | solution.py:27
  166.1 14.1 %collective-permute-start.12 = (bf16[192,512]{1,0:T(8,128)(2,1)S(1)}, bf16[192,512]{1,0:T(8,128)(2,1)S(1)}, u32[]{:S(2)}, u32[]{:S(2)}) collective-permute-start(bf16[192,512]{1,0:T(8,128)(2,1)S(1)} %bitcast.44), channel_id=1, source_target_pairs={{0,32},{16,48},{32,0},{48,16},{1,33},{17,49},{33,1},{49,17},{2,34}... | collective-permute-start | bytes 589832 | tf_op jit(solution)/shard_map/ppermute | solution.py:27
  175.7 19.7 %collective-permute-start.20 = (bf16[96,3072]{1,0:T(8,128)(2,1)S(1)}, bf16[96,3072]{1,0:T(8,128)(2,1)S(1)}, u32[]{:S(2)}, u32[]{:S(2)}) collective-permute-start(bf16[96,3072]{1,0:T(8,128)(2,1)S(1)} %slice.198), channel_id=1, source_target_pairs={{0,32},{16,48},{32,0},{48,16},{1,33},{17,49},{33,1},{49,17},{2,34}... | collective-permute-start | bytes 1769480 | tf_op jit(solution)/shard_map/ppermute | solution.py:27
  177.3 17.3 %collective-permute-start.14 = (bf16[192,512]{1,0:T(8,128)(2,1)S(1)}, bf16[192,512]{1,0:T(8,128)(2,1)S(1)}, u32[]{:S(2)}, u32[]{:S(2)}) collective-permute-start(bf16[192,512]{1,0:T(8,128)(2,1)S(1)} %bitcast.46), channel_id=1, source_target_pairs={{0,16},{16,0},{32,48},{48,32},{1,17},{17,1},{33,49},{49,33},{2,18}... | collective-permute-start | bytes 589832 | tf_op jit(solution)/shard_map/ppermute | solution.py:27
  195.5 1.0 copy-start.9
  196.5 7.8 %collective-permute-start.15 = (bf16[384,512]{1,0:T(8,128)(2,1)S(1)}, bf16[384,512]{1,0:T(8,128)(2,1)S(1)}, u32[]{:S(2)}, u32[]{:S(2)}) collective-permute-start(bf16[384,512]{1,0:T(8,128)(2,1)S(1)} %copy-done.9), channel_id=1, source_target_pairs={{0,32},{16,48},{32,0},{48,16},{1,33},{17,49},{33,1},{49,17},{2,34}... | collective-permute-start | bytes 1179656 | tf_op jit(solution)/shard_map/ppermute | solution.py:27
  196.6 17.2 %copy-start.7 = (bf16[96,6144]{1,0:T(8,128)(2,1)}, bf16[96,6144]{1,0:T(8,128)(2,1)S(1)}, u32[]{:S(2)}) copy-start(bf16[96,6144]{1,0:T(8,128)(2,1)S(1)} %slice_dynamic-update-slice_fusion) | copy-start | bytes 3538948
Sparse Core Ops, SparseCore 0:
  21.7 47.9 all-gather.2
  71.5 43.6 all-gather.4
  117.7 45.3 reduce-scatter.2
  165.6 46.0 reduce-scatter.4

commit v2 on v1

--- a/solution.py
+++ b/solution.py
@@ -35,6 +35,21 @@
     return lax.ppermute(a, "c", [(0, 1), (1, 0)])
 
 
+def gather4(swap, own):
+    return [own] + [swap(own, m) for m in (1, 2, 3)]
+
+
+def scatter4(swap, blocks):
+    total = blocks[0].astype(f32)
+    for m in (1, 3, 2):
+        total = total + swap(blocks[m], m).astype(f32)
+    return total.astype(bf16)
+
+
+def add(a, b):
+    return (a.astype(f32) + b.astype(f32)).astype(bf16)
+
+
 def near4(swap, own):
     return swap(own, 1), swap(own, 3)
 
@@ -42,10 +57,6 @@
 def far4(swap, near1, near3):
     half = near1.shape[0] // 2
     return swap(near1[:half], 3), swap(near3[half:], 1)
-
-
-def add(a, b):
-    return (a.astype(f32) + b.astype(f32)).astype(bf16)
 
 
 def scatter_far(swap, far):
@@ -103,49 +114,41 @@
     hid = gelu_value(pre32).astype(bf16)
     low, high = hid[:, :384], hid[:, 384:]
     keep, give = jnp.where(yl == 0, low, high), jnp.where(yl == 0, high, low)
-    hidden = [lax.all_gather(keep, "z", axis=1, tiled=True)]
     got_h = swap_y(give, 1)
-    hidden.append(lax.all_gather(got_h, "z", axis=1, tiled=True))
 
-    keep, give = split_columns(down_weight, yl)
-    own = jnp.concatenate([keep, swap_y(give, 1)], axis=0)
-    near = near4(swap_x, own)
+    keep_w, give_w = split_columns(after(down_weight, give), yl)
+    got_w = swap_y(give_w, 1)
+    hidden = lax.all_gather(jnp.concatenate([keep, after(got_h, keep_w)], axis=0), "z", axis=1, tiled=True)
+    own = jnp.concatenate([keep_w, got_w], axis=0)
+    near = near4(swap_x, after(own, got_h))
     weight = jnp.concatenate([own, near[0], *far4(swap_x, *near), near[1]], axis=0)
 
-    small = grad_out.T
-    got = [small] + [swap_y(small, m) for m in (1, 2, 3)]
+    got = gather4(swap_y, after(grad_out.T, near[0]))
     part = jnp.stack([jnp.concatenate([got[2 * h], got[2 * h + 1]], axis=1) for h in range(2)])
     table = jnp.concatenate([part, swap_c(part)], axis=0).reshape(8, 96, 1024)
     flip = x ^ (yh * 2 + c)
     iota = jnp.arange(8, dtype=jnp.int32)
     place = flip ^ (iota >> 1)
     grads = table[(place & 1) * 4 + (place >> 1) * 2 + (yl ^ (iota & 1))].reshape(768, 1024)
-    grads = [grads[:, :512], grads[:, 512:]]
 
-    gh = []
-    for t in (1, 0):
-        part = lax.dot_general(weight, grads[t], (((0,), (0,)), ((), ())), preferred_element_type=f32).astype(bf16)
-        part = after(part, hidden[1], *gh)
-        gh.append(lax.psum_scatter(part, "z", scatter_dimension=0, tiled=True))
-    mine, theirs = gh[1].T, swap_y(gh[0], 1).T
-    grad_hidden = join_columns(mine, theirs, yl)
+    gh = lax.dot_general(weight, grads, (((0,), (0,)), ((), ())), preferred_element_type=f32).astype(bf16)
+    gh_z = lax.psum_scatter(after(gh, hidden), "z", scatter_dimension=0, tiled=True)
+    grad_hidden = join_columns(gh_z[:, :512].T, swap_y(gh_z[:, 512:], 1).T, yl)
     grad_pre = (grad_hidden.astype(f32) * gelu_slope(pre32)).astype(bf16)
 
-    gw = sum(jnp.dot(grads[t], hidden[t], preferred_element_type=f32) for t in range(2))
-    gw = gw.astype(bf16).reshape(4, 192, 3072)
-    sent = scatter_far(swap_x, gw[2])
-    total = add3(gw[0], *scatter_near(swap_x, gw[1], gw[3], *sent)).astype(bf16)
+    gw_all = jnp.dot(after(grads, gh), hidden, preferred_element_type=f32).astype(bf16)
+    gw = gw_all.reshape(4, 192, 3072)
+    far = scatter_far(swap_x, gw[2])
+    near = scatter_near(swap_x, gw[1], gw[3], *far)
+    order = (flip ^ (((iota >> 1) & 1) * 2 + (iota >> 2))) * 2 + ((iota & 1) ^ yl)
+    out = lax.dot_general(weight, after(hidden, gw_all, *far), (((1,), (1,)), ((), ())), preferred_element_type=f32)
+    out = out.astype(bf16).reshape(8, 96, 1024)
+    part = add(out[order[:4]], swap_c(out[order[4:]])).reshape(2, 192, 1024)
+    output = scatter4(swap_y, [part[m >> 1, :, (m & 1) * 512 : (m & 1) * 512 + 512] for m in range(4)])
+
+    total = add3(after(gw[0], output), *near).astype(bf16)
     grad_weight = join_columns(total[:96], swap_y(total[96:], 1), yl)
-
-    order = (flip ^ (((iota >> 1) & 1) * 2 + (iota >> 2))) * 2 + ((iota & 1) ^ yl)
-    total = jnp.zeros((192, 512), f32)
-    for t in (1, 0):
-        out = lax.dot_general(weight, after(hidden[t], gw), (((1,), (1,)), ((), ())), preferred_element_type=f32)
-        out = out.astype(bf16).reshape(8, 96, 512)
-        part = add(out[order[:4]], swap_c(out[order[4:]])).reshape(2, 192, 512)
-        for h in (1, 0):
-            total = total + (swap_y(part[h], 2 * h + t) if h + t else part[h]).astype(f32)
-    output = total.astype(bf16).T
+    output = output.T
     return output, grad_pre, grad_weight
 
 

time: 222 us -> 209 us (0.941)
  local copies, waits for them, and re-layouts: 25.8 us -> 14.3 us
  matrix products: 31.6 us -> 24.5 us
  waiting for transfers between devices: 104 us -> 110 us
    ppermute x8, waiting for transfers between devices: 33.8 us -> 48.2 us  [swap_x(): return lax.ppermute(a, 'x', [(i, i ^ mask) for i in range(4)])]
    reduce_scatter x2 -> x1, waiting for transfers between devices: 12.1 us -> 0.02 us  [shards(): lax.psum_scatter(after(gh, hidden), 'z', scatter_dimension=0, tiled=True)]
    ppermute x10, waiting for transfers between devices: 47.2 us -> 55.5 us  [swap_y(): return lax.ppermute(a, ('yl', 'yh'), [(i, i ^ flip) for i in range(4)])]
    dot_general x6 -> x3, matrix products: 31.6 us -> 24.5 us  [the longest x1 9.18 us: shards(): lax.dot_general(weight, grads, (((0,), (0,)), ((), ())), preferred_elemen...]
    all_gather x2 -> x1, waiting for transfers between devices: 10 us -> 5.82 us  [shards(): lax.all_gather(jnp.concatenate([keep, after(got_h, keep_w)], axis=0), 'z'...]
    gather x4 -> x2, local copies, waits for them, and re-layouts: 5.34 us -> 2.07 us  [shards(): part = add(out[order[:4]], swap_c(out[order[4:]])).reshape(2, 192, 1024)]
    unnamed x41 -> x44, local copies, waits for them, and re-layouts: 11.5 us -> 9.01 us
    concatenate x1, local copies, waits for them, and re-layouts: 2.38 us -> 0.08 us  [shards(): jnp.concatenate([own, near[0], *far4(swap_x, *near), near[1]], axis=0)]
  transfers between devices with their start and end apart: 25 -> 22, of which waited for: 17 -> 16; matrix products, arithmetic and copies ran while one was open for 29% -> 20% of each run, Pallas kernels for 1% -> 1%
where the time goes in v2:
time: 209 us; the launch traced here: 208 us
  waiting for transfers between devices  110 us (53%)
  starting transfers between devices  28.5 us (14%)
  matrix products  24.5 us (12%)
  between operations  14.5 us (7%)
  local copies, waits for them, and re-layouts  14.3 us (7%)
  other arithmetic  14.1 us (7%)
  Pallas kernels  2.4 us (1%)
    ppermute x10, waiting for transfers between devices, swap_y(): return lax.ppermute(a, ('yl', 'yh'), [(i, i ^ flip) for i in range(4)])  55.5 us
    ppermute x8, waiting for transfers between devices, swap_x(): return lax.ppermute(a, 'x', [(i, i ^ mask) for i in range(4)])  48.2 us
    ppermute x10, starting transfers between devices, swap_y(): return lax.ppermute(a, ('yl', 'yh'), [(i, i ^ flip) for i in range(4)])  15.4 us
    ppermute x8, starting transfers between devices, swap_x(): return lax.ppermute(a, 'x', [(i, i ^ mask) for i in range(4)])  12.8 us
    dot_general x1, matrix products, shards(): lax.dot_general(weight, grads, (((0,), (0,)), ((), ())), preferred_elemen...  9.18 us
    unnamed x44, local copies, waits for them, and re-layouts  9.01 us
    dot_general x1, matrix products, shards(): jnp.dot(after(grads, gh), hidden, preferred_element_type=f32).astype(bf16)  8.25 us
    dot_general x1, matrix products, shards(): lax.dot_general(weight, after(hidden, gw_all, *far), (((1,), (1,)), ((),...  7.05 us
  transfers between devices with their start and end apart: 22, of which 16 were waited for; matrix products, arithmetic and copies ran while one was open for 20% of the time, Pallas kernels for 1%

profile of v2, /device:TPU:2, one launch (start us, length us, event | category | flops | bytes accessed | tf_op | source)
XLA Modules:
  0.0 207.7 jit_solution(6042044860384475634)
XLA Ops:
  7.2 1.4 copy.6
  8.6 0.5 fusion.2
  9.2 1.7 collective-permute-start.1
  10.9 2.4 %shard_map.58 = (bf16[96,3072]{1,0:T(8,128)(2,1)}, bf16[96,3072]{1,0:T(8,128)(2,1)}) custom-call(s32[1]{0:T(128)} %bitcast.which_ref, bf16[96,6144]{1,0:T(8,128)(2,1)} %a_ref), custom_call_target="tpu_custom_call" | custom-call | bytes 2359296 | tf_op jit(solution)/shard_map/pallas_call | solution.py:95
  13.3 6.9 %collective-permute-done.1 = bf16[512,384]{0,1:T(8,128)(2,1)S(1)} collective-permute-done((bf16[512,384]{0,1:T(8,128)(2,1)S(1)}, bf16[512,384]{0,1:T(8,128)(2,1)S(1)}, u32[]{:S(2)}, u32[]{:S(2)}) %collective-permute-start.1) | collective-permute-done | bytes 393248 | tf_op jit(solution)/shard_map/ppermute | solution.py:27
  20.2 1.0 pad_maximum_fusion.4
  21.3 1.7 collective-permute-start
  22.9 12.6 %collective-permute-done = bf16[96,3072]{1,0:T(8,128)(2,1)S(1)} collective-permute-done((bf16[96,3072]{1,0:T(8,128)(2,1)S(1)}, bf16[96,3072]{1,0:T(8,128)(2,1)S(1)}, u32[]{:S(2)}, u32[]{:S(2)}) %collective-permute-start) | collective-permute-done | bytes 589856 | tf_op jit(solution)/shard_map/ppermute | solution.py:27
  35.6 1.2 pad_maximum_fusion.1
  36.8 0.2 collective-permute-start.2
  37.0 2.5 %collective-permute-start.4 = (bf16[192,3072]{1,0:T(8,128)(2,1)}, bf16[192,3072]{1,0:T(8,128)(2,1)S(1)}, u32[]{:S(2)}, u32[]{:S(2)}) collective-permute-start(bf16[192,3072]{1,0:T(8,128)(2,1)} %pad_maximum_fusion.1), channel_id=1, source_target_pairs={{0,192},{64,128},{128,64},{192,0},{1,193},{65,129},{129,65},{193,1... | collective-permute-start | bytes 3538952 | tf_op jit(solution)/shard_map/ppermute | solution.py:31
  39.5 1.2 constant_dynamic-update-slice_fusion.5
  40.8 22.1 %collective-permute-done.2 = bf16[192,3072]{1,0:T(8,128)(2,1)S(1)} collective-permute-done((bf16[192,3072]{1,0:T(8,128)(2,1)}, bf16[192,3072]{1,0:T(8,128)(2,1)S(1)}, u32[]{:S(2)}, u32[]{:S(2)}) %collective-permute-start.2) | collective-permute-done | bytes 1179680 | tf_op jit(solution)/shard_map/ppermute | solution.py:31
  62.9 3.0 %collective-permute-start.8 = (bf16[192,512]{1,0:T(8,128)(2,1)S(1)}, bf16[192,512]{1,0:T(8,128)(2,1)S(1)}, u32[]{:S(2)}, u32[]{:S(2)}) collective-permute-start(bf16[192,512]{1,0:T(8,128)(2,1)S(1)} %bitcast.41), channel_id=1, source_target_pairs={{0,48},{16,32},{32,16},{48,0},{1,49},{17,33},{33,17},{49,1},{2,50}... | collective-permute-start | bytes 589832 | tf_op jit(solution)/shard_map/ppermute | solution.py:27
  65.9 0.6 collective-permute-start.7
  66.6 0.5 collective-permute-start.6
  67.1 0.4 collective-permute-start.5
  67.5 2.5 %collective-permute-start.3 = (bf16[96,3072]{1,0:T(8,128)(2,1)S(1)}, bf16[96,3072]{1,0:T(8,128)(2,1)S(1)}, u32[]{:S(2)}, u32[]{:S(2)}) collective-permute-start(bf16[96,3072]{1,0:T(8,128)(2,1)S(1)} %slice.172), channel_id=1, source_target_pairs={{0,192},{64,128},{128,64},{192,0},{1,193},{65,129},{129,65},{193,1... | collective-permute-start | bytes 1769480 | tf_op jit(solution)/shard_map/ppermute | solution.py:31
  70.1 3.1 %collective-permute-done.6 = bf16[192,512]{1,0:T(8,128)(2,1)S(1)} collective-permute-done((bf16[192,512]{1,0:T(8,128)(2,1)S(1)}, bf16[192,512]{1,0:T(8,128)(2,1)S(1)}, u32[]{:S(2)}, u32[]{:S(2)}) %collective-permute-start.6) | collective-permute-done | bytes 196640 | tf_op jit(solution)/shard_map/ppermute | solution.py:27
  73.2 0.1 collective-permute-done.7
  73.4 0.3 collective-permute-start.9
  73.7 5.9 %collective-permute-done.3 = bf16[96,3072]{1,0:T(8,128)(2,1)S(1)} collective-permute-done((bf16[96,3072]{1,0:T(8,128)(2,1)S(1)}, bf16[96,3072]{1,0:T(8,128)(2,1)S(1)}, u32[]{:S(2)}, u32[]{:S(2)}) %collective-permute-start.3) | collective-permute-done | bytes 589856 | tf_op jit(solution)/shard_map/ppermute | solution.py:31
  79.7 0.1 constant_dynamic-update-slice_fusion
  79.8 0.2 pad_maximum_fusion
  80.0 2.0 copy-done.7
  82.0 1.8 gather_fusion
  83.8 9.2 %convolution_convert_fusion = bf16[3072,1024]{1,0:T(8,128)(2,1)} fusion(bf16[768,3072]{1,0:T(8,128)(2,1)} %copy-done.7, bf16[768,1024]{1,0:T(8,128)(2,1)} %bitcast.39), kind=kOutput, calls=%fused_computation.3 | convolution fusion | flops 4834983936 | bytes 12582912 | tf_op jit(solution)/shard_map/dot_general | solution.py:134
  93.0 5.8 %all-gather.2.cloned.1.call-done = bf16[1024,3072]{0,1:T(8,128)(2,1)} async-done(((bf16[1024,384]{0,1:T(8,128)(2,1)}), bf16[1024,3072]{0,1:T(8,128)(2,1)}) %all-gather.2.cloned.1.call-update) | async-done | bytes 6291472 | tf_op jit(solution)/shard_map/all_gather | solution.py:121
  98.8 8.2 %convolution_convert_fusion.1 = bf16[768,3072]{1,0:T(8,128)(2,1)S(1)} fusion(bf16[768,1024]{1,0:T(8,128)(2,1)S(1)} %bitcast.40, bf16[1024,3072]{0,1:T(8,128)(2,1)} %all-gather.2.cloned.1.call-done), kind=kOutput, calls=%fused_computation.4 | convolution fusion | flops 4834197504 | bytes 12582912 | tf_op jit(solution)/shard_map/dot_general | solution.py:139
  107.1 0.2 fusion.21
  107.3 1.9 copy-done
  109.2 1.5 collective-permute-start.11
  110.7 1.8 collective-permute-start.10
  112.5 11.7 %collective-permute-done.11 = bf16[96,3072]{1,0:T(8,128)(2,1)S(1)} collective-permute-done((bf16[96,3072]{1,0:T(8,128)(2,1)S(1)}, bf16[96,3072]{1,0:T(8,128)(2,1)S(1)}, u32[]{:S(2)}, u32[]{:S(2)}) %collective-permute-start.11) | collective-permute-done | bytes 589856 | tf_op jit(solution)/shard_map/ppermute | solution.py:31
  124.3 0.8 copy-done.5
  125.1 0.5 collective-permute-done.10
  125.6 7.1 %convolution_convert_fusion.2 = bf16[768,1024]{1,0:T(8,128)(2,1)S(1)} fusion(bf16[768,3072]{1,0:T(8,128)(2,1)} %copy-done.7, bf16[1024,3072]{0,1:T(8,128)(2,1)S(1)} %copy-done.9), kind=kOutput, calls=%fused_computation.15 | convolution fusion | flops 4832624640 | bytes 12582912 | tf_op jit(solution)/shard_map/dot_general | solution.py:144
  132.7 1.5 gather_fusion.2
  134.1 2.0 add_convert_fusion.3
  136.2 1.1 pad_maximum_fusion.3
  137.3 0.9 collective-permute-start.18
  138.2 1.1 pad_maximum_fusion.2
  139.2 3.1 %collective-permute-start.17 = (bf16[192,3072]{1,0:T(8,128)(2,1)}, bf16[192,3072]{1,0:T(8,128)(2,1)}, u32[]{:S(2)}, u32[]{:S(2)}) collective-permute-start(bf16[192,3072]{1,0:T(8,128)(2,1)} %pad_maximum_fusion.2), channel_id=1, source_target_pairs={{0,64},{64,0},{128,192},{192,128},{1,65},{65,1},{129,193},{193,129... | collective-permute-start | bytes 3538952 | tf_op jit(solution)/shard_map/ppermute | solution.py:31
  142.3 0.6 gather_fusion.1
  142.9 1.5 add_convert_fusion.1
  144.5 1.6 collective-permute-start.13
  146.0 2.7 %collective-permute-start.15 = (bf16[192,512]{1,0:T(8,128)(2,1)S(1)}, bf16[192,512]{1,0:T(8,128)(2,1)S(1)}, u32[]{:S(2)}, u32[]{:S(2)}) collective-permute-start(bf16[192,512]{1,0:T(8,128)(2,1)S(1)} %get-tuple-element.37), channel_id=1, source_target_pairs={{0,16},{16,0},{32,48},{48,32},{1,17},{17,1},{33,49},{49,33},{2,18}... | collective-permute-start | bytes 589832 | tf_op jit(solution)/shard_map/ppermute | solution.py:27
  148.8 0.5 collective-permute-start.14
  149.2 3.1 %collective-permute-done.13 = bf16[192,512]{1,0:T(8,128)(2,1)S(1)} collective-permute-done((bf16[192,512]{1,0:T(8,128)(2,1)S(1)}, bf16[192,512]{1,0:T(8,128)(2,1)S(1)}, u32[]{:S(2)}, u32[]{:S(2)}) %collective-permute-start.13) | collective-permute-done | bytes 196640 | tf_op jit(solution)/shard_map/ppermute | solution.py:27
  152.3 5.4 %collective-permute-done.15 = bf16[192,512]{1,0:T(8,128)(2,1)S(1)} collective-permute-done((bf16[192,512]{1,0:T(8,128)(2,1)S(1)}, bf16[192,512]{1,0:T(8,128)(2,1)S(1)}, u32[]{:S(2)}, u32[]{:S(2)}) %collective-permute-start.15) | collective-permute-done | bytes 196640 | tf_op jit(solution)/shard_map/ppermute | solution.py:27
  157.8 2.6 %collective-permute-done.14 = bf16[192,512]{1,0:T(8,128)(2,1)S(1)} collective-permute-done((bf16[192,512]{1,0:T(8,128)(2,1)S(1)}, bf16[192,512]{1,0:T(8,128)(2,1)S(1)}, u32[]{:S(2)}, u32[]{:S(2)}) %collective-permute-start.14) | collective-permute-done | bytes 196640 | tf_op jit(solution)/shard_map/ppermute | solution.py:27
  160.3 0.8 fusion.13
  161.1 4.9 %collective-permute-done.18 = bf16[192,3072]{1,0:T(8,128)(2,1)} collective-permute-done((bf16[192,3072]{1,0:T(8,128)(2,1)}, bf16[192,3072]{1,0:T(8,128)(2,1)}, u32[]{:S(2)}, u32[]{:S(2)}) %collective-permute-start.18) | collective-permute-done | bytes 1179680 | tf_op jit(solution)/shard_map/ppermute | solution.py:31
  166.0 3.0 %collective-permute-done.17 = bf16[192,3072]{1,0:T(8,128)(2,1)} collective-permute-done((bf16[192,3072]{1,0:T(8,128)(2,1)}, bf16[192,3072]{1,0:T(8,128)(2,1)}, u32[]{:S(2)}, u32[]{:S(2)}) %collective-permute-start.17) | collective-permute-done | bytes 1179680 | tf_op jit(solution)/shard_map/ppermute | solution.py:31
  169.0 2.2 %add_convert_fusion = bf16[192,3072]{1,0:T(8,128)(2,1)S(1)} fusion(bf16[192,3072]{1,0:T(8,128)(2,1)} %collective-permute-done.18, bf16[192,3072]{1,0:T(8,128)(2,1)} %collective-permute-done.17, bf16[192,3072]{1,0:T(8,128)(2,1)S(1)} %slice-done), kind=kLoop, calls=%fused_computation.12 | loop fusion | flops 3538944 | bytes 4718592 | tf_op jit(solution)/shard_map/convert_element_type | solution.py:149
  171.2 1.6 collective-permute-start.19
  172.8 13.4 %collective-permute-done.19 = bf16[96,3072]{1,0:T(8,128)(2,1)S(1)} collective-permute-done((bf16[96,3072]{1,0:T(8,128)(2,1)S(1)}, bf16[96,3072]{1,0:T(8,128)(2,1)S(1)}, u32[]{:S(2)}, u32[]{:S(2)}) %collective-permute-start.19) | collective-permute-done | bytes 589856 | tf_op jit(solution)/shard_map/ppermute | solution.py:27
  186.2 0.1 broadcast_select_fusion
  186.6 1.0 slice.181
  187.7 1.6 collective-permute-start.16
  189.3 8.3 %collective-permute-done.16 = bf16[384,512]{1,0:T(8,128)(2,1)S(1)} collective-permute-done((bf16[384,512]{1,0:T(8,128)(2,1)S(1)}, bf16[384,512]{1,0:T(8,128)(2,1)S(1)}, u32[]{:S(2)}, u32[]{:S(2)}) %collective-permute-start.16) | collective-permute-done | bytes 393248 | tf_op jit(solution)/shard_map/ppermute | solution.py:27
  197.5 1.1 select_bitcast_fusion.1
  198.6 1.1 fusion.7
  199.7 1.2 copy.7
  (66 shorter events, 1.2 us)
Async XLA Ops:
  7.2 91.6 %all-gather.2.cloned.1.call-start = ((), (), s32[]{:S(2)}) async-start(), calls=%async_computation.1 | async-start | bytes 7077888 | tf_op jit(solution)/shard_map/all_gather | solution.py:121
  9.2 10.9 %collective-permute-start.1 = (bf16[512,384]{0,1:T(8,128)(2,1)S(1)}, bf16[512,384]{0,1:T(8,128)(2,1)S(1)}, u32[]{:S(2)}, u32[]{:S(2)}) collective-permute-start(bf16[512,384]{0,1:T(8,128)(2,1)S(1)} %get-tuple-element.40), channel_id=1, source_target_pairs={{0,32},{16,48},{32,0},{48,16},{1,33},{17,49},{33,1},{49,17},{2,34}... | collective-permute-start | bytes 1179656 | tf_op jit(solution)/shard_map/ppermute | solution.py:27
  13.3 7.9 %copy-start.10 = (bf16[96,3072]{1,0:T(8,128)(2,1)S(1)}, bf16[96,3072]{1,0:T(8,128)(2,1)}, u32[]{:S(2)}) copy-start(bf16[96,3072]{1,0:T(8,128)(2,1)} %get-tuple-element.15) | copy-start | bytes 1769476
  13.3 22.2 %copy-start.1 = (bf16[96,3072]{1,0:T(8,128)(2,1)S(1)}, bf16[96,3072]{1,0:T(8,128)(2,1)}, u32[]{:S(2)}) copy-start(bf16[96,3072]{1,0:T(8,128)(2,1)} %get-tuple-element.14) | copy-start | bytes 1769476
  21.2 165.4 %reduce-scatter.2.cloned.1.call-start = ((), (), s32[]{:S(2)}) async-start(), calls=%async_computation.2 | async-start | bytes 7077888 | tf_op jit(solution)/shard_map/reduce_scatter | solution.py:135
  21.3 14.3 %collective-permute-start = (bf16[96,3072]{1,0:T(8,128)(2,1)S(1)}, bf16[96,3072]{1,0:T(8,128)(2,1)S(1)}, u32[]{:S(2)}, u32[]{:S(2)}) collective-permute-start(bf16[96,3072]{1,0:T(8,128)(2,1)S(1)} %copy-done.10), channel_id=1, source_target_pairs={{0,32},{16,48},{32,0},{48,16},{1,33},{17,49},{33,1},{49,17},{2,34}... | collective-permute-start | bytes 1769480 | tf_op jit(solution)/shard_map/ppermute | solution.py:27
  35.5 1.2 copy-start.2
  36.8 26.1 %copy-start.6 = (bf16[512,192]{0,1:T(8,128)(2,1)S(1)}, bf16[512,192]{0,1:T(8,128)(2,1)}, u32[]{:S(2)}) copy-start(bf16[512,192]{0,1:T(8,128)(2,1)} %param.5) | copy-start | bytes 589828
  36.8 26.1 %collective-permute-start.2 = (bf16[192,3072]{1,0:T(8,128)(2,1)}, bf16[192,3072]{1,0:T(8,128)(2,1)S(1)}, u32[]{:S(2)}, u32[]{:S(2)}) collective-permute-start(bf16[192,3072]{1,0:T(8,128)(2,1)} %pad_maximum_fusion.1), channel_id=1, source_target_pairs={{0,64},{64,0},{128,192},{192,128},{1,65},{65,1},{129,193},{193,129... | collective-permute-start | bytes 3538952 | tf_op jit(solution)/shard_map/ppermute | solution.py:31
  37.0 30.0 %collective-permute-start.4 = (bf16[192,3072]{1,0:T(8,128)(2,1)}, bf16[192,3072]{1,0:T(8,128)(2,1)S(1)}, u32[]{:S(2)}, u32[]{:S(2)}) collective-permute-start(bf16[192,3072]{1,0:T(8,128)(2,1)} %pad_maximum_fusion.1), channel_id=1, source_target_pairs={{0,192},{64,128},{128,64},{192,0},{1,193},{65,129},{129,65},{193,1... | collective-permute-start | bytes 3538952 | tf_op jit(solution)/shard_map/ppermute | solution.py:31
  39.5 1.2 copy-start.3
  62.9 10.2 %collective-permute-start.8 = (bf16[192,512]{1,0:T(8,128)(2,1)S(1)}, bf16[192,512]{1,0:T(8,128)(2,1)S(1)}, u32[]{:S(2)}, u32[]{:S(2)}) collective-permute-start(bf16[192,512]{1,0:T(8,128)(2,1)S(1)} %bitcast.41), channel_id=1, source_target_pairs={{0,48},{16,32},{32,16},{48,0},{1,49},{17,33},{33,17},{49,1},{2,50}... | collective-permute-start | bytes 589832 | tf_op jit(solution)/shard_map/ppermute | solution.py:27
  65.9 7.4 %collective-permute-start.7 = (bf16[192,512]{1,0:T(8,128)(2,1)S(1)}, bf16[192,512]{1,0:T(8,128)(2,1)S(1)}, u32[]{:S(2)}, u32[]{:S(2)}) collective-permute-start(bf16[192,512]{1,0:T(8,128)(2,1)S(1)} %bitcast.42), channel_id=1, source_target_pairs={{0,16},{16,0},{32,48},{48,32},{1,17},{17,1},{33,49},{49,33},{2,18}... | collective-permute-start | bytes 589832 | tf_op jit(solution)/shard_map/ppermute | solution.py:27
  66.6 6.5 %collective-permute-start.6 = (bf16[192,512]{1,0:T(8,128)(2,1)S(1)}, bf16[192,512]{1,0:T(8,128)(2,1)S(1)}, u32[]{:S(2)}, u32[]{:S(2)}) collective-permute-start(bf16[192,512]{1,0:T(8,128)(2,1)S(1)} %bitcast.43), channel_id=1, source_target_pairs={{0,32},{16,48},{32,0},{48,16},{1,33},{17,49},{33,1},{49,17},{2,34}... | collective-permute-start | bytes 589832 | tf_op jit(solution)/shard_map/ppermute | solution.py:27
  67.1 12.6 %collective-permute-start.5 = (bf16[96,3072]{1,0:T(8,128)(2,1)S(1)}, bf16[96,3072]{1,0:T(8,128)(2,1)S(1)}, u32[]{:S(2)}, u32[]{:S(2)}) collective-permute-start(bf16[96,3072]{1,0:T(8,128)(2,1)S(1)} %slice.173), channel_id=1, source_target_pairs={{0,64},{64,0},{128,192},{192,128},{1,65},{65,1},{129,193},{193,129... | collective-permute-start | bytes 1769480 | tf_op jit(solution)/shard_map/ppermute | solution.py:31
  67.5 12.1 %collective-permute-start.3 = (bf16[96,3072]{1,0:T(8,128)(2,1)S(1)}, bf16[96,3072]{1,0:T(8,128)(2,1)S(1)}, u32[]{:S(2)}, u32[]{:S(2)}) collective-permute-start(bf16[96,3072]{1,0:T(8,128)(2,1)S(1)} %slice.172), channel_id=1, source_target_pairs={{0,192},{64,128},{128,64},{192,0},{1,193},{65,129},{129,65},{193,1... | collective-permute-start | bytes 1769480 | tf_op jit(solution)/shard_map/ppermute | solution.py:31
  73.4 6.4 %collective-permute-start.9 = (bf16[2,192,1024]{2,1,0:T(8,128)(2,1)S(1)}, bf16[2,192,1024]{2,1,0:T(8,128)(2,1)S(1)}, u32[]{:S(2)}, u32[]{:S(2)}) collective-permute-start(bf16[2,192,1024]{2,1,0:T(8,128)(2,1)S(1)} %pad_maximum_fusion.5), channel_id=1, source_target_pairs={{0,8},{8,0},{1,9},{9,1},{2,10},{10,2},{3,11},{11,3},{4,12},{12,4},... | collective-permute-start | bytes 2359304 | tf_op jit(solution)/shard_map/ppermute | solution.py:35
  79.8 2.2 %copy-start.7 = (bf16[768,3072]{1,0:T(8,128)(2,1)}, bf16[768,3072]{1,0:T(8,128)(2,1)S(1)}, u32[]{:S(2)}) copy-start(bf16[768,3072]{1,0:T(8,128)(2,1)S(1)} %constant_dynamic-update-slice_fusion) | copy-start | bytes 14155780
  93.0 5.9 %copy-start.4 = (bf16[8,96,1024]{2,1,0:T(8,128)(2,1)S(1)}, bf16[8,96,1024]{2,1,0:T(8,128)(2,1)}, u32[]{:S(2)}) copy-start(bf16[8,96,1024]{2,1,0:T(8,128)(2,1)} %gather_fusion) | copy-start | bytes 4718596
  98.8 26.8 %copy-start.9 = (bf16[1024,3072]{0,1:T(8,128)(2,1)S(1)}, bf16[1024,3072]{0,1:T(8,128)(2,1)}, u32[]{:S(2)}) copy-start(bf16[1024,3072]{0,1:T(8,128)(2,1)} %all-gather.2.cloned.1.call-done) | copy-start | bytes 18874372
  107.1 2.1 %copy-start = (bf16[768,3072]{1,0:T(8,128)(2,1)}, bf16[768,3072]{1,0:T(8,128)(2,1)S(1)}, u32[]{:S(2)}) copy-start(bf16[768,3072]{1,0:T(8,128)(2,1)S(1)} %convolution_convert_fusion.1) | copy-start | bytes 14155780
  109.2 15.1 %collective-permute-start.11 = (bf16[96,3072]{1,0:T(8,128)(2,1)S(1)}, bf16[96,3072]{1,0:T(8,128)(2,1)S(1)}, u32[]{:S(2)}, u32[]{:S(2)}) collective-permute-start(bf16[96,3072]{1,0:T(8,128)(2,1)S(1)} %get-tuple-element.28), channel_id=1, source_target_pairs={{0,192},{64,128},{128,64},{192,0},{1,193},{65,129},{129,65},{193,1... | collective-permute-start | bytes 1769480 | tf_op jit(solution)/shard_map/ppermute | solution.py:31
  110.7 14.9 %collective-permute-start.10 = (bf16[96,3072]{1,0:T(8,128)(2,1)S(1)}, bf16[96,3072]{1,0:T(8,128)(2,1)}, u32[]{:S(2)}, u32[]{:S(2)}) collective-permute-start(bf16[96,3072]{1,0:T(8,128)(2,1)S(1)} %get-tuple-element.29), channel_id=1, source_target_pairs={{0,64},{64,0},{128,192},{192,128},{1,65},{65,1},{129,193},{193,129... | collective-permute-start | bytes 1769480 | tf_op jit(solution)/shard_map/ppermute | solution.py:31
  124.3 0.8 copy-start.5
  134.1 8.8 %collective-permute-start.12 = (bf16[4,96,1024]{2,1,0:T(8,128)(2,1)}, bf16[4,96,1024]{2,1,0:T(8,128)(2,1)}, u32[]{:S(2)}, u32[]{:S(2)}) collective-permute-start(bf16[4,96,1024]{2,1,0:T(8,128)(2,1)} %gather_fusion.2), channel_id=1, source_target_pairs={{0,8},{8,0},{1,9},{9,1},{2,10},{10,2},{3,11},{11,3},{4,12},{12,4},... | collective-permute-start | bytes 2359304 | tf_op jit(solution)/shard_map/ppermute | solution.py:35
  137.3 28.7 %collective-permute-start.18 = (bf16[192,3072]{1,0:T(8,128)(2,1)}, bf16[192,3072]{1,0:T(8,128)(2,1)}, u32[]{:S(2)}, u32[]{:S(2)}) collective-permute-start(bf16[192,3072]{1,0:T(8,128)(2,1)} %pad_maximum_fusion.3), channel_id=1, source_target_pairs={{0,192},{64,128},{128,64},{192,0},{1,193},{65,129},{129,65},{193,1... | collective-permute-start | bytes 3538952 | tf_op jit(solution)/shard_map/ppermute | solution.py:31
  139.2 29.7 %collective-permute-start.17 = (bf16[192,3072]{1,0:T(8,128)(2,1)}, bf16[192,3072]{1,0:T(8,128)(2,1)}, u32[]{:S(2)}, u32[]{:S(2)}) collective-permute-start(bf16[192,3072]{1,0:T(8,128)(2,1)} %pad_maximum_fusion.2), channel_id=1, source_target_pairs={{0,64},{64,0},{128,192},{192,128},{1,65},{65,1},{129,193},{193,129... | collective-permute-start | bytes 3538952 | tf_op jit(solution)/shard_map/ppermute | solution.py:31
  144.5 7.9 %collective-permute-start.13 = (bf16[192,512]{1,0:T(8,128)(2,1)S(1)}, bf16[192,512]{1,0:T(8,128)(2,1)S(1)}, u32[]{:S(2)}, u32[]{:S(2)}) collective-permute-start(bf16[192,512]{1,0:T(8,128)(2,1)S(1)} %get-tuple-element.36), channel_id=1, source_target_pairs={{0,32},{16,48},{32,0},{48,16},{1,33},{17,49},{33,1},{49,17},{2,34}... | collective-permute-start | bytes 589832 | tf_op jit(solution)/shard_map/ppermute | solution.py:27
  146.0 11.7 %collective-permute-start.15 = (bf16[192,512]{1,0:T(8,128)(2,1)S(1)}, bf16[192,512]{1,0:T(8,128)(2,1)S(1)}, u32[]{:S(2)}, u32[]{:S(2)}) collective-permute-start(bf16[192,512]{1,0:T(8,128)(2,1)S(1)} %get-tuple-element.37), channel_id=1, source_target_pairs={{0,16},{16,0},{32,48},{48,32},{1,17},{17,1},{33,49},{49,33},{2,18}... | collective-permute-start | bytes 589832 | tf_op jit(solution)/shard_map/ppermute | solution.py:27
  148.7 20.2 %slice-start = ((bf16[768,3072]{1,0:T(8,128)(2,1)}), bf16[192,3072]{1,0:T(8,128)(2,1)S(1)}, s32[]{:S(2)}) async-start(bf16[768,3072]{1,0:T(8,128)(2,1)} %copy-done), calls=%async_computation.3 | async-start | bytes 2359296 | tf_op jit(solution)/shard_map/slice | solution.py:149
  148.8 11.6 %collective-permute-start.14 = (bf16[192,512]{1,0:T(8,128)(2,1)S(1)}, bf16[192,512]{1,0:T(8,128)(2,1)S(1)}, u32[]{:S(2)}, u32[]{:S(2)}) collective-permute-start(bf16[192,512]{1,0:T(8,128)(2,1)S(1)} %get-tuple-element.38), channel_id=1, source_target_pairs={{0,48},{16,32},{32,16},{48,0},{1,49},{17,33},{33,17},{49,1},{2,50}... | collective-permute-start | bytes 589832 | tf_op jit(solution)/shard_map/ppermute | solution.py:27
  171.2 15.0 %collective-permute-start.19 = (bf16[96,3072]{1,0:T(8,128)(2,1)S(1)}, bf16[96,3072]{1,0:T(8,128)(2,1)S(1)}, u32[]{:S(2)}, u32[]{:S(2)}) collective-permute-start(bf16[96,3072]{1,0:T(8,128)(2,1)S(1)} %slice.188), channel_id=1, source_target_pairs={{0,32},{16,48},{32,0},{48,16},{1,33},{17,49},{33,1},{49,17},{2,34}... | collective-permute-start | bytes 1769480 | tf_op jit(solution)/shard_map/ppermute | solution.py:27
  187.7 9.9 %collective-permute-start.16 = (bf16[384,512]{1,0:T(8,128)(2,1)S(1)}, bf16[384,512]{1,0:T(8,128)(2,1)S(1)}, u32[]{:S(2)}, u32[]{:S(2)}) collective-permute-start(bf16[384,512]{1,0:T(8,128)(2,1)S(1)} %slice.181), channel_id=1, source_target_pairs={{0,32},{16,48},{32,0},{48,16},{1,33},{17,49},{33,1},{49,17},{2,34}... | collective-permute-start | bytes 1179656 | tf_op jit(solution)/shard_map/ppermute | solution.py:27
  189.3 10.5 %copy-start.8 = (bf16[96,6144]{1,0:T(8,128)(2,1)}, bf16[96,6144]{1,0:T(8,128)(2,1)S(1)}, u32[]{:S(2)}) copy-start(bf16[96,6144]{1,0:T(8,128)(2,1)S(1)} %slice_dynamic-update-slice_fusion) | copy-start | bytes 3538948
Sparse Core Ops, SparseCore 0:
  21.3 77.4 all-gather.1
  101.3 73.6 reduce-scatter.1

commit v3 on v2

--- a/solution.py
+++ b/solution.py
@@ -64,11 +64,11 @@
     return swap(far[:half], 1), swap(far[half:], 3)
 
 
-def scatter_near(swap, near1, near3, far1, far3):
+def scatter_near(near1, near3, far1, far3):
     half = far1.shape[0]
     near3 = jnp.concatenate([add(near3[:half], far1), near3[half:]], axis=0)
     near1 = jnp.concatenate([near1[:half], add(near1[half:], far3)], axis=0)
-    return swap(near1, 1), swap(near3, 3)
+    return near1, near3
 
 
 def add3(own, got1, got3):
@@ -132,22 +132,23 @@
     grads = table[(place & 1) * 4 + (place >> 1) * 2 + (yl ^ (iota & 1))].reshape(768, 1024)
 
     gh = lax.dot_general(weight, grads, (((0,), (0,)), ((), ())), preferred_element_type=f32).astype(bf16)
-    gh_z = lax.psum_scatter(after(gh, hidden), "z", scatter_dimension=0, tiled=True)
-    grad_hidden = join_columns(gh_z[:, :512].T, swap_y(gh_z[:, 512:], 1).T, yl)
+    gh = lax.psum_scatter(after(gh, hidden), "z", scatter_dimension=0, tiled=True)
+    theirs = swap_y(gh[:, 512:], 1)
+    grad_hidden = join_columns(gh[:, :512].T, theirs.T, yl)
     grad_pre = (grad_hidden.astype(f32) * gelu_slope(pre32)).astype(bf16)
 
-    gw_all = jnp.dot(after(grads, gh), hidden, preferred_element_type=f32).astype(bf16)
+    gw_all = jnp.dot(grads, hidden, preferred_element_type=f32).astype(bf16)
     gw = gw_all.reshape(4, 192, 3072)
     far = scatter_far(swap_x, gw[2])
-    near = scatter_near(swap_x, gw[1], gw[3], *far)
+    out = lax.dot_general(weight, after(hidden, gw_all), (((1,), (1,)), ((), ())), preferred_element_type=f32)
+    out = out.astype(bf16).reshape(8, 96, 1024)
+    passed = scatter_near(gw[1], gw[3], after(far[0], out), after(far[1], out))
+    near = swap_x(passed[0], 1), swap_x(passed[1], 3)
     order = (flip ^ (((iota >> 1) & 1) * 2 + (iota >> 2))) * 2 + ((iota & 1) ^ yl)
-    out = lax.dot_general(weight, after(hidden, gw_all, *far), (((1,), (1,)), ((), ())), preferred_element_type=f32)
-    out = out.astype(bf16).reshape(8, 96, 1024)
     part = add(out[order[:4]], swap_c(out[order[4:]])).reshape(2, 192, 1024)
     output = scatter4(swap_y, [part[m >> 1, :, (m & 1) * 512 : (m & 1) * 512 + 512] for m in range(4)])
-
     total = add3(after(gw[0], output), *near).astype(bf16)
-    grad_weight = join_columns(total[:96], swap_y(total[96:], 1), yl)
+    grad_weight = join_columns(after(total[:96], theirs), swap_y(total[96:], 1), yl)
     output = output.T
     return output, grad_pre, grad_weight
 

time: 209 us -> 198 us (0.947)
  waiting for transfers between devices: 110 us -> 101 us
    ppermute x10, waiting for transfers between devices: 55.5 us -> 39.3 us  [swap_y(): return lax.ppermute(a, ('yl', 'yh'), [(i, i ^ flip) for i in range(4)])]
    reduce_scatter x1, waiting for transfers between devices: 0.02 us -> 12.4 us  [shards(): lax.psum_scatter(after(gh, hidden), 'z', scatter_dimension=0, tiled=True)]
    ppermute x8, waiting for transfers between devices: 48.2 us -> 43.8 us  [swap_x(): return lax.ppermute(a, 'x', [(i, i ^ mask) for i in range(4)])]
  transfers between devices with their start and end apart: 22 -> 22, of which waited for: 16 -> 16; matrix products, arithmetic and copies ran while one was open for 20% -> 22% of each run, Pallas kernels for 1% -> 1%
where the time goes in v3:
time: 198 us; the launch traced here: 197 us
  waiting for transfers between devices  101 us (51%)
  starting transfers between devices  28 us (14%)
  matrix products  24.4 us (12%)
  local copies, waits for them, and re-layouts  14.7 us (7%)
  between operations  14.4 us (7%)
  other arithmetic  13.1 us (7%)
  Pallas kernels  2.4 us (1%)
    ppermute x8, waiting for transfers between devices, swap_x(): return lax.ppermute(a, 'x', [(i, i ^ mask) for i in range(4)])  43.8 us
    ppermute x10, waiting for transfers between devices, swap_y(): return lax.ppermute(a, ('yl', 'yh'), [(i, i ^ flip) for i in range(4)])  39.3 us
    ppermute x10, starting transfers between devices, swap_y(): return lax.ppermute(a, ('yl', 'yh'), [(i, i ^ flip) for i in range(4)])  15 us
    ppermute x8, starting transfers between devices, swap_x(): return lax.ppermute(a, 'x', [(i, i ^ mask) for i in range(4)])  12.6 us
    reduce_scatter x1, waiting for transfers between devices, shards(): lax.psum_scatter(after(gh, hidden), 'z', scatter_dimension=0, tiled=True)  12.4 us
    dot_general x1, matrix products, shards(): lax.dot_general(weight, grads, (((0,), (0,)), ((), ())), preferred_elemen...  9.14 us
    dot_general x1, matrix products, shards(): gw_all = jnp.dot(grads, hidden, preferred_element_type=f32).astype(bf16)  8.25 us
    unnamed x44, local copies, waits for them, and re-layouts  8.16 us
  transfers between devices with their start and end apart: 22, of which 16 were waited for; matrix products, arithmetic and copies ran while one was open for 22% of the time, Pallas kernels for 1%

profile of v3, /device:TPU:2, one launch (start us, length us, event | category | flops | bytes accessed | tf_op | source)
XLA Modules:
  0.0 197.5 jit_solution(8993791749533673950)
XLA Ops:
  7.2 1.4 copy.6
  8.6 0.5 fusion.2
  9.2 1.7 collective-permute-start.1
  10.9 2.4 %shard_map.58 = (bf16[96,3072]{1,0:T(8,128)(2,1)}, bf16[96,3072]{1,0:T(8,128)(2,1)}) custom-call(s32[1]{0:T(128)} %bitcast.which_ref, bf16[96,6144]{1,0:T(8,128)(2,1)} %a_ref), custom_call_target="tpu_custom_call" | custom-call | bytes 2359296 | tf_op jit(solution)/shard_map/pallas_call | solution.py:95
  13.3 6.9 %collective-permute-done.1 = bf16[512,384]{0,1:T(8,128)(2,1)S(1)} collective-permute-done((bf16[512,384]{0,1:T(8,128)(2,1)S(1)}, bf16[512,384]{0,1:T(8,128)(2,1)S(1)}, u32[]{:S(2)}, u32[]{:S(2)}) %collective-permute-start.1) | collective-permute-done | bytes 393248 | tf_op jit(solution)/shard_map/ppermute | solution.py:27
  20.2 1.0 pad_maximum_fusion.4
  21.3 1.7 collective-permute-start
  22.9 12.6 %collective-permute-done = bf16[96,3072]{1,0:T(8,128)(2,1)S(1)} collective-permute-done((bf16[96,3072]{1,0:T(8,128)(2,1)S(1)}, bf16[96,3072]{1,0:T(8,128)(2,1)S(1)}, u32[]{:S(2)}, u32[]{:S(2)}) %collective-permute-start) | collective-permute-done | bytes 589856 | tf_op jit(solution)/shard_map/ppermute | solution.py:27
  35.6 1.2 pad_maximum_fusion.1
  36.8 0.2 collective-permute-start.2
  37.0 2.5 %collective-permute-start.4 = (bf16[192,3072]{1,0:T(8,128)(2,1)}, bf16[192,3072]{1,0:T(8,128)(2,1)S(1)}, u32[]{:S(2)}, u32[]{:S(2)}) collective-permute-start(bf16[192,3072]{1,0:T(8,128)(2,1)} %pad_maximum_fusion.1), channel_id=1, source_target_pairs={{0,192},{64,128},{128,64},{192,0},{1,193},{65,129},{129,65},{193,1... | collective-permute-start | bytes 3538952 | tf_op jit(solution)/shard_map/ppermute | solution.py:31
  39.5 1.2 constant_dynamic-update-slice_fusion.5
  40.8 22.1 %collective-permute-done.2 = bf16[192,3072]{1,0:T(8,128)(2,1)S(1)} collective-permute-done((bf16[192,3072]{1,0:T(8,128)(2,1)}, bf16[192,3072]{1,0:T(8,128)(2,1)S(1)}, u32[]{:S(2)}, u32[]{:S(2)}) %collective-permute-start.2) | collective-permute-done | bytes 1179680 | tf_op jit(solution)/shard_map/ppermute | solution.py:31
  62.9 3.2 %collective-permute-start.7 = (bf16[192,512]{1,0:T(8,128)(2,1)S(1)}, bf16[192,512]{1,0:T(8,128)(2,1)S(1)}, u32[]{:S(2)}, u32[]{:S(2)}) collective-permute-start(bf16[192,512]{1,0:T(8,128)(2,1)S(1)} %bitcast.41), channel_id=1, source_target_pairs={{0,16},{16,0},{32,48},{48,32},{1,17},{17,1},{33,49},{49,33},{2,18}... | collective-permute-start | bytes 589832 | tf_op jit(solution)/shard_map/ppermute | solution.py:27
  66.1 1.1 collective-permute-start.8
  67.2 1.6 collective-permute-start.3
  68.8 1.9 collective-permute-start.5
  70.7 0.1 constant_dynamic-update-slice_fusion.3
  70.8 2.2 %collective-permute-done.6 = bf16[192,512]{1,0:T(8,128)(2,1)S(1)} collective-permute-done((bf16[192,512]{1,0:T(8,128)(2,1)S(1)}, bf16[192,512]{1,0:T(8,128)(2,1)S(1)}, u32[]{:S(2)}, u32[]{:S(2)}) %collective-permute-start.6) | collective-permute-done | bytes 196640 | tf_op jit(solution)/shard_map/ppermute | solution.py:27
  73.1 0.5 collective-permute-done.8
  73.8 0.3 collective-permute-start.9
  74.0 5.2 %collective-permute-done.3 = bf16[96,3072]{1,0:T(8,128)(2,1)S(1)} collective-permute-done((bf16[96,3072]{1,0:T(8,128)(2,1)S(1)}, bf16[96,3072]{1,0:T(8,128)(2,1)S(1)}, u32[]{:S(2)}, u32[]{:S(2)}) %collective-permute-start.3) | collective-permute-done | bytes 589856 | tf_op jit(solution)/shard_map/ppermute | solution.py:31
  79.3 1.4 collective-permute-done.5
  80.7 0.1 constant_dynamic-update-slice_fusion
  80.8 0.2 pad_maximum_fusion
  80.9 2.0 %copy-done.7 = bf16[768,3072]{1,0:T(8,128)(2,1)} copy-done((bf16[768,3072]{1,0:T(8,128)(2,1)}, bf16[768,3072]{1,0:T(8,128)(2,1)S(1)}, u32[]{:S(2)}) %copy-start.7) | copy-done | bytes 4718616
  82.9 1.8 gather_fusion
  84.7 9.1 %convolution_convert_fusion = bf16[3072,1024]{1,0:T(8,128)(2,1)} fusion(bf16[768,3072]{1,0:T(8,128)(2,1)} %copy-done.7, bf16[768,1024]{1,0:T(8,128)(2,1)} %bitcast.39), kind=kOutput, calls=%fused_computation.3 | convolution fusion | flops 4834983936 | bytes 12582912 | tf_op jit(solution)/shard_map/dot_general | solution.py:134
  93.9 4.9 %all-gather.2.cloned.1.call-done = bf16[1024,3072]{0,1:T(8,128)(2,1)} async-done(((bf16[1024,384]{0,1:T(8,128)(2,1)}), bf16[1024,3072]{0,1:T(8,128)(2,1)}) %all-gather.2.cloned.1.call-update) | async-done | bytes 6291472 | tf_op jit(solution)/shard_map/all_gather | solution.py:121
  98.9 8.3 %convolution_convert_fusion.1 = bf16[768,3072]{1,0:T(8,128)(2,1)S(1)} fusion(bf16[768,1024]{1,0:T(8,128)(2,1)S(1)} %bitcast.40, bf16[1024,3072]{0,1:T(8,128)(2,1)} %all-gather.2.cloned.1.call-done), kind=kOutput, calls=%fused_computation.4 | convolution fusion | flops 4834197504 | bytes 12582912 | tf_op jit(solution)/shard_map/dot_general | solution.py:140
  107.2 1.3 fusion.21
  108.5 1.1 copy-done
  109.6 0.6 collective-permute-start.17
  110.2 2.1 %collective-permute-start.15 = (bf16[96,3072]{1,0:T(8,128)(2,1)}, bf16[96,3072]{1,0:T(8,128)(2,1)}, u32[]{:S(2)}, u32[]{:S(2)}) collective-permute-start(bf16[96,3072]{1,0:T(8,128)(2,1)} %get-tuple-element.33), channel_id=1, source_target_pairs={{0,192},{64,128},{128,64},{192,0},{1,193},{65,129},{129,65},{193,1... | collective-permute-start | bytes 1769480 | tf_op jit(solution)/shard_map/ppermute | solution.py:31
  112.3 7.0 %convolution_convert_fusion.2 = bf16[768,1024]{1,0:T(8,128)(2,1)S(1)} fusion(bf16[768,3072]{1,0:T(8,128)(2,1)} %copy-done.7, bf16[1024,3072]{0,1:T(8,128)(2,1)S(1)} %copy-done.9), kind=kOutput, calls=%fused_computation.15 | convolution fusion | flops 4832624640 | bytes 12582912 | tf_op jit(solution)/shard_map/dot_general | solution.py:143
  119.3 1.5 gather_fusion.2
  120.8 4.2 %collective-permute-done.17 = bf16[96,3072]{1,0:T(8,128)(2,1)} collective-permute-done((bf16[96,3072]{1,0:T(8,128)(2,1)}, bf16[96,3072]{1,0:T(8,128)(2,1)}, u32[]{:S(2)}, u32[]{:S(2)}) %collective-permute-start.17) | collective-permute-done | bytes 589856 | tf_op jit(solution)/shard_map/ppermute | solution.py:31
  125.0 0.6 collective-permute-done.15
  125.6 2.0 %add_convert_fusion.3 = (bf16[96,3072]{1,0:T(8,128)(2,1)S(1)}, bf16[96,3072]{1,0:T(8,128)(2,1)S(1)}) fusion(bf16[96,3072]{1,0:T(8,128)(2,1)} %collective-permute-done.15, bf16[768,3072]{1,0:T(8,128)(2,1)} %copy-done, bf16[96,3072]{1,0:T(8,128)(2,1)} %collective-permute-done.17), kind=kLoop, calls=%fused_computation.31 | loop fusion | flops 2359296 | bytes 3538944 | tf_op jit(solution)/shard_map/convert_element_type | solution.py:50
  127.7 1.1 pad_maximum_fusion.2
  128.8 2.3 %collective-permute-start.16 = (bf16[192,3072]{1,0:T(8,128)(2,1)}, bf16[192,3072]{1,0:T(8,128)(2,1)}, u32[]{:S(2)}, u32[]{:S(2)}) collective-permute-start(bf16[192,3072]{1,0:T(8,128)(2,1)} %pad_maximum_fusion.2), channel_id=1, source_target_pairs={{0,64},{64,0},{128,192},{192,128},{1,65},{65,1},{129,193},{193,129... | collective-permute-start | bytes 3538952 | tf_op jit(solution)/shard_map/ppermute | solution.py:31
  131.1 1.1 pad_maximum_fusion.3
  132.2 1.5 collective-permute-start.18
  133.6 0.6 gather_fusion.1
  134.3 1.4 add_convert_fusion.1
  135.8 1.6 collective-permute-start.11
  137.3 2.1 %collective-permute-start.12 = (bf16[192,512]{1,0:T(8,128)(2,1)S(1)}, bf16[192,512]{1,0:T(8,128)(2,1)S(1)}, u32[]{:S(2)}, u32[]{:S(2)}) collective-permute-start(bf16[192,512]{1,0:T(8,128)(2,1)S(1)} %get-tuple-element.44), channel_id=1, source_target_pairs={{0,48},{16,32},{32,16},{48,0},{1,49},{17,33},{33,17},{49,1},{2,50}... | collective-permute-start | bytes 589832 | tf_op jit(solution)/shard_map/ppermute | solution.py:27
  139.4 0.6 collective-permute-start.13
  140.1 3.4 %collective-permute-done.11 = bf16[192,512]{1,0:T(8,128)(2,1)S(1)} collective-permute-done((bf16[192,512]{1,0:T(8,128)(2,1)S(1)}, bf16[192,512]{1,0:T(8,128)(2,1)S(1)}, u32[]{:S(2)}, u32[]{:S(2)}) %collective-permute-start.11) | collective-permute-done | bytes 196640 | tf_op jit(solution)/shard_map/ppermute | solution.py:27
  143.5 4.3 %collective-permute-done.12 = bf16[192,512]{1,0:T(8,128)(2,1)S(1)} collective-permute-done((bf16[192,512]{1,0:T(8,128)(2,1)S(1)}, bf16[192,512]{1,0:T(8,128)(2,1)S(1)}, u32[]{:S(2)}, u32[]{:S(2)}) %collective-permute-start.12) | collective-permute-done | bytes 196640 | tf_op jit(solution)/shard_map/ppermute | solution.py:27
  147.7 0.8 fusion.13
  148.5 7.7 %collective-permute-done.16 = bf16[192,3072]{1,0:T(8,128)(2,1)} collective-permute-done((bf16[192,3072]{1,0:T(8,128)(2,1)}, bf16[192,3072]{1,0:T(8,128)(2,1)}, u32[]{:S(2)}, u32[]{:S(2)}) %collective-permute-start.16) | collective-permute-done | bytes 1179680 | tf_op jit(solution)/shard_map/ppermute | solution.py:31
  156.2 2.6 %collective-permute-done.18 = bf16[192,3072]{1,0:T(8,128)(2,1)} collective-permute-done((bf16[192,3072]{1,0:T(8,128)(2,1)}, bf16[192,3072]{1,0:T(8,128)(2,1)}, u32[]{:S(2)}, u32[]{:S(2)}) %collective-permute-start.18) | collective-permute-done | bytes 1179680 | tf_op jit(solution)/shard_map/ppermute | solution.py:31
  158.7 2.2 %add_convert_fusion = bf16[192,3072]{1,0:T(8,128)(2,1)S(1)} fusion(bf16[192,3072]{1,0:T(8,128)(2,1)} %collective-permute-done.18, bf16[192,3072]{1,0:T(8,128)(2,1)} %collective-permute-done.16, bf16[192,3072]{1,0:T(8,128)(2,1)S(1)} %slice-done), kind=kLoop, calls=%fused_computation.12 | loop fusion | flops 3538944 | bytes 4718592 | tf_op jit(solution)/shard_map/convert_element_type | solution.py:150
  161.0 0.1 fusion.22
  161.0 1.6 collective-permute-start.19
  162.6 12.4 %reduce-scatter.2.cloned.1.call-done = bf16[384,1024]{1,0:T(8,128)(2,1)} async-done(((bf16[3072,1024]{1,0:T(8,128)(2,1)}), bf16[384,1024]{1,0:T(8,128)(2,1)}) %reduce-scatter.2.cloned.1.call-update) | async-done | bytes 786448 | tf_op jit(solution)/shard_map/reduce_scatter | solution.py:135
  175.1 1.0 slice.179
  176.1 1.6 collective-permute-start.14
  177.7 9.4 %collective-permute-done.14 = bf16[384,512]{1,0:T(8,128)(2,1)S(1)} collective-permute-done((bf16[384,512]{1,0:T(8,128)(2,1)S(1)}, bf16[384,512]{1,0:T(8,128)(2,1)S(1)}, u32[]{:S(2)}, u32[]{:S(2)}) %collective-permute-start.14) | collective-permute-done | bytes 393248 | tf_op jit(solution)/shard_map/ppermute | solution.py:27
  187.1 0.1 broadcast_select_fusion
  187.5 0.8 copy-done.5
  188.4 1.1 fusion.7
  189.5 1.2 copy.7
  (66 shorter events, 1.1 us)
Async XLA Ops:
  7.2 91.6 %all-gather.2.cloned.1.call-start = ((), (), s32[]{:S(2)}) async-start(), calls=%async_computation.1 | async-start | bytes 7077888 | tf_op jit(solution)/shard_map/all_gather | solution.py:121
  9.2 10.9 %collective-permute-start.1 = (bf16[512,384]{0,1:T(8,128)(2,1)S(1)}, bf16[512,384]{0,1:T(8,128)(2,1)S(1)}, u32[]{:S(2)}, u32[]{:S(2)}) collective-permute-start(bf16[512,384]{0,1:T(8,128)(2,1)S(1)} %get-tuple-element.46), channel_id=1, source_target_pairs={{0,32},{16,48},{32,0},{48,16},{1,33},{17,49},{33,1},{49,17},{2,34}... | collective-permute-start | bytes 1179656 | tf_op jit(solution)/shard_map/ppermute | solution.py:27
  13.3 7.9 %copy-start.10 = (bf16[96,3072]{1,0:T(8,128)(2,1)S(1)}, bf16[96,3072]{1,0:T(8,128)(2,1)}, u32[]{:S(2)}) copy-start(bf16[96,3072]{1,0:T(8,128)(2,1)} %get-tuple-element.17) | copy-start | bytes 1769476
  13.3 22.2 %copy-start.1 = (bf16[96,3072]{1,0:T(8,128)(2,1)S(1)}, bf16[96,3072]{1,0:T(8,128)(2,1)}, u32[]{:S(2)}) copy-start(bf16[96,3072]{1,0:T(8,128)(2,1)} %get-tuple-element.16) | copy-start | bytes 1769476
  21.2 153.9 %reduce-scatter.2.cloned.1.call-start = ((), (), s32[]{:S(2)}) async-start(), calls=%async_computation.2 | async-start | bytes 7077888 | tf_op jit(solution)/shard_map/reduce_scatter | solution.py:135
  21.3 14.3 %collective-permute-start = (bf16[96,3072]{1,0:T(8,128)(2,1)S(1)}, bf16[96,3072]{1,0:T(8,128)(2,1)S(1)}, u32[]{:S(2)}, u32[]{:S(2)}) collective-permute-start(bf16[96,3072]{1,0:T(8,128)(2,1)S(1)} %copy-done.10), channel_id=1, source_target_pairs={{0,32},{16,48},{32,0},{48,16},{1,33},{17,49},{33,1},{49,17},{2,34}... | collective-permute-start | bytes 1769480 | tf_op jit(solution)/shard_map/ppermute | solution.py:27
  35.5 1.2 copy-start.2
  36.8 26.1 %copy-start.6 = (bf16[512,192]{0,1:T(8,128)(2,1)S(1)}, bf16[512,192]{0,1:T(8,128)(2,1)}, u32[]{:S(2)}) copy-start(bf16[512,192]{0,1:T(8,128)(2,1)} %param.5) | copy-start | bytes 589828
  36.8 26.1 %collective-permute-start.2 = (bf16[192,3072]{1,0:T(8,128)(2,1)}, bf16[192,3072]{1,0:T(8,128)(2,1)S(1)}, u32[]{:S(2)}, u32[]{:S(2)}) collective-permute-start(bf16[192,3072]{1,0:T(8,128)(2,1)} %pad_maximum_fusion.1), channel_id=1, source_target_pairs={{0,64},{64,0},{128,192},{192,128},{1,65},{65,1},{129,193},{193,129... | collective-permute-start | bytes 3538952 | tf_op jit(solution)/shard_map/ppermute | solution.py:31
  37.0 31.8 %collective-permute-start.4 = (bf16[192,3072]{1,0:T(8,128)(2,1)}, bf16[192,3072]{1,0:T(8,128)(2,1)S(1)}, u32[]{:S(2)}, u32[]{:S(2)}) collective-permute-start(bf16[192,3072]{1,0:T(8,128)(2,1)} %pad_maximum_fusion.1), channel_id=1, source_target_pairs={{0,192},{64,128},{128,64},{192,0},{1,193},{65,129},{129,65},{193,1... | collective-permute-start | bytes 3538952 | tf_op jit(solution)/shard_map/ppermute | solution.py:31
  39.5 1.2 copy-start.3
  62.9 10.2 %collective-permute-start.7 = (bf16[192,512]{1,0:T(8,128)(2,1)S(1)}, bf16[192,512]{1,0:T(8,128)(2,1)S(1)}, u32[]{:S(2)}, u32[]{:S(2)}) collective-permute-start(bf16[192,512]{1,0:T(8,128)(2,1)S(1)} %bitcast.41), channel_id=1, source_target_pairs={{0,16},{16,0},{32,48},{48,32},{1,17},{17,1},{33,49},{49,33},{2,18}... | collective-permute-start | bytes 589832 | tf_op jit(solution)/shard_map/ppermute | solution.py:27
  66.1 7.5 %collective-permute-start.8 = (bf16[192,512]{1,0:T(8,128)(2,1)S(1)}, bf16[192,512]{1,0:T(8,128)(2,1)S(1)}, u32[]{:S(2)}, u32[]{:S(2)}) collective-permute-start(bf16[192,512]{1,0:T(8,128)(2,1)S(1)} %bitcast.42), channel_id=1, source_target_pairs={{0,48},{16,32},{32,16},{48,0},{1,49},{17,33},{33,17},{49,1},{2,50}... | collective-permute-start | bytes 589832 | tf_op jit(solution)/shard_map/ppermute | solution.py:27
  67.2 5.9 %collective-permute-start.6 = (bf16[192,512]{1,0:T(8,128)(2,1)S(1)}, bf16[192,512]{1,0:T(8,128)(2,1)S(1)}, u32[]{:S(2)}, u32[]{:S(2)}) collective-permute-start(bf16[192,512]{1,0:T(8,128)(2,1)S(1)} %bitcast.43), channel_id=1, source_target_pairs={{0,32},{16,48},{32,0},{48,16},{1,33},{17,49},{33,1},{49,17},{2,34}... | collective-permute-start | bytes 589832 | tf_op jit(solution)/shard_map/ppermute | solution.py:27
  67.2 12.0 %collective-permute-start.3 = (bf16[96,3072]{1,0:T(8,128)(2,1)S(1)}, bf16[96,3072]{1,0:T(8,128)(2,1)S(1)}, u32[]{:S(2)}, u32[]{:S(2)}) collective-permute-start(bf16[96,3072]{1,0:T(8,128)(2,1)S(1)} %slice.172), channel_id=1, source_target_pairs={{0,192},{64,128},{128,64},{192,0},{1,193},{65,129},{129,65},{193,1... | collective-permute-start | bytes 1769480 | tf_op jit(solution)/shard_map/ppermute | solution.py:31
  68.8 11.8 %collective-permute-start.5 = (bf16[96,3072]{1,0:T(8,128)(2,1)S(1)}, bf16[96,3072]{1,0:T(8,128)(2,1)S(1)}, u32[]{:S(2)}, u32[]{:S(2)}) collective-permute-start(bf16[96,3072]{1,0:T(8,128)(2,1)S(1)} %slice.173), channel_id=1, source_target_pairs={{0,64},{64,0},{128,192},{192,128},{1,65},{65,1},{129,193},{193,129... | collective-permute-start | bytes 1769480 | tf_op jit(solution)/shard_map/ppermute | solution.py:31
  73.8 7.0 %collective-permute-start.9 = (bf16[2,192,1024]{2,1,0:T(8,128)(2,1)S(1)}, bf16[2,192,1024]{2,1,0:T(8,128)(2,1)S(1)}, u32[]{:S(2)}, u32[]{:S(2)}) collective-permute-start(bf16[2,192,1024]{2,1,0:T(8,128)(2,1)S(1)} %pad_maximum_fusion.5), channel_id=1, source_target_pairs={{0,8},{8,0},{1,9},{9,1},{2,10},{10,2},{3,11},{11,3},{4,12},{12,4},... | collective-permute-start | bytes 2359304 | tf_op jit(solution)/shard_map/ppermute | solution.py:35
  80.7 2.2 %copy-start.7 = (bf16[768,3072]{1,0:T(8,128)(2,1)}, bf16[768,3072]{1,0:T(8,128)(2,1)S(1)}, u32[]{:S(2)}) copy-start(bf16[768,3072]{1,0:T(8,128)(2,1)S(1)} %constant_dynamic-update-slice_fusion) | copy-start | bytes 14155780
  93.9 5.0 %copy-start.4 = (bf16[8,96,1024]{2,1,0:T(8,128)(2,1)S(1)}, bf16[8,96,1024]{2,1,0:T(8,128)(2,1)}, u32[]{:S(2)}) copy-start(bf16[8,96,1024]{2,1,0:T(8,128)(2,1)} %gather_fusion) | copy-start | bytes 4718596
  98.9 13.4 %copy-start.9 = (bf16[1024,3072]{0,1:T(8,128)(2,1)S(1)}, bf16[1024,3072]{0,1:T(8,128)(2,1)}, u32[]{:S(2)}) copy-start(bf16[1024,3072]{0,1:T(8,128)(2,1)} %all-gather.2.cloned.1.call-done) | copy-start | bytes 18874372
  107.2 2.5 %copy-start = (bf16[768,3072]{1,0:T(8,128)(2,1)}, bf16[768,3072]{1,0:T(8,128)(2,1)S(1)}, u32[]{:S(2)}) copy-start(bf16[768,3072]{1,0:T(8,128)(2,1)S(1)} %convolution_convert_fusion.1) | copy-start | bytes 14155780
  109.6 15.4 %collective-permute-start.17 = (bf16[96,3072]{1,0:T(8,128)(2,1)}, bf16[96,3072]{1,0:T(8,128)(2,1)}, u32[]{:S(2)}, u32[]{:S(2)}) collective-permute-start(bf16[96,3072]{1,0:T(8,128)(2,1)} %get-tuple-element.32), channel_id=1, source_target_pairs={{0,64},{64,0},{128,192},{192,128},{1,65},{65,1},{129,193},{193,129... | collective-permute-start | bytes 1769480 | tf_op jit(solution)/shard_map/ppermute | solution.py:31
  110.2 15.4 %collective-permute-start.15 = (bf16[96,3072]{1,0:T(8,128)(2,1)}, bf16[96,3072]{1,0:T(8,128)(2,1)}, u32[]{:S(2)}, u32[]{:S(2)}) collective-permute-start(bf16[96,3072]{1,0:T(8,128)(2,1)} %get-tuple-element.33), channel_id=1, source_target_pairs={{0,192},{64,128},{128,64},{192,0},{1,193},{65,129},{129,65},{193,1... | collective-permute-start | bytes 1769480 | tf_op jit(solution)/shard_map/ppermute | solution.py:31
  120.8 13.5 %collective-permute-start.10 = (bf16[4,96,1024]{2,1,0:T(8,128)(2,1)}, bf16[4,96,1024]{2,1,0:T(8,128)(2,1)}, u32[]{:S(2)}, u32[]{:S(2)}) collective-permute-start(bf16[4,96,1024]{2,1,0:T(8,128)(2,1)} %gather_fusion.2), channel_id=1, source_target_pairs={{0,8},{8,0},{1,9},{9,1},{2,10},{10,2},{3,11},{11,3},{4,12},{12,4},... | collective-permute-start | bytes 2359304 | tf_op jit(solution)/shard_map/ppermute | solution.py:35
  128.8 27.4 %collective-permute-start.16 = (bf16[192,3072]{1,0:T(8,128)(2,1)}, bf16[192,3072]{1,0:T(8,128)(2,1)}, u32[]{:S(2)}, u32[]{:S(2)}) collective-permute-start(bf16[192,3072]{1,0:T(8,128)(2,1)} %pad_maximum_fusion.2), channel_id=1, source_target_pairs={{0,64},{64,0},{128,192},{192,128},{1,65},{65,1},{129,193},{193,129... | collective-permute-start | bytes 3538952 | tf_op jit(solution)/shard_map/ppermute | solution.py:31
  132.2 26.6 %collective-permute-start.18 = (bf16[192,3072]{1,0:T(8,128)(2,1)}, bf16[192,3072]{1,0:T(8,128)(2,1)}, u32[]{:S(2)}, u32[]{:S(2)}) collective-permute-start(bf16[192,3072]{1,0:T(8,128)(2,1)} %pad_maximum_fusion.3), channel_id=1, source_target_pairs={{0,192},{64,128},{128,64},{192,0},{1,193},{65,129},{129,65},{193,1... | collective-permute-start | bytes 3538952 | tf_op jit(solution)/shard_map/ppermute | solution.py:31
  135.8 7.7 %collective-permute-start.11 = (bf16[192,512]{1,0:T(8,128)(2,1)S(1)}, bf16[192,512]{1,0:T(8,128)(2,1)S(1)}, u32[]{:S(2)}, u32[]{:S(2)}) collective-permute-start(bf16[192,512]{1,0:T(8,128)(2,1)S(1)} %get-tuple-element.42), channel_id=1, source_target_pairs={{0,32},{16,48},{32,0},{48,16},{1,33},{17,49},{33,1},{49,17},{2,34}... | collective-permute-start | bytes 589832 | tf_op jit(solution)/shard_map/ppermute | solution.py:27
  137.3 10.4 %collective-permute-start.12 = (bf16[192,512]{1,0:T(8,128)(2,1)S(1)}, bf16[192,512]{1,0:T(8,128)(2,1)S(1)}, u32[]{:S(2)}, u32[]{:S(2)}) collective-permute-start(bf16[192,512]{1,0:T(8,128)(2,1)S(1)} %get-tuple-element.44), channel_id=1, source_target_pairs={{0,48},{16,32},{32,16},{48,0},{1,49},{17,33},{33,17},{49,1},{2,50}... | collective-permute-start | bytes 589832 | tf_op jit(solution)/shard_map/ppermute | solution.py:27
  139.4 19.3 %slice-start = ((bf16[768,3072]{1,0:T(8,128)(2,1)}), bf16[192,3072]{1,0:T(8,128)(2,1)S(1)}, s32[]{:S(2)}) async-start(bf16[768,3072]{1,0:T(8,128)(2,1)} %copy-done), calls=%async_computation.3 | async-start | bytes 2359296 | tf_op jit(solution)/shard_map/slice | solution.py:150
  139.4 8.3 %collective-permute-start.13 = (bf16[192,512]{1,0:T(8,128)(2,1)S(1)}, bf16[192,512]{1,0:T(8,128)(2,1)S(1)}, u32[]{:S(2)}, u32[]{:S(2)}) collective-permute-start(bf16[192,512]{1,0:T(8,128)(2,1)S(1)} %get-tuple-element.43), channel_id=1, source_target_pairs={{0,16},{16,0},{32,48},{48,32},{1,17},{17,1},{33,49},{49,33},{2,18}... | collective-permute-start | bytes 589832 | tf_op jit(solution)/shard_map/ppermute | solution.py:27
  161.0 26.1 %collective-permute-start.19 = (bf16[96,3072]{1,0:T(8,128)(2,1)S(1)}, bf16[96,3072]{1,0:T(8,128)(2,1)S(1)}, u32[]{:S(2)}, u32[]{:S(2)}) collective-permute-start(bf16[96,3072]{1,0:T(8,128)(2,1)S(1)} %get-tuple-element.38), channel_id=1, source_target_pairs={{0,32},{16,48},{32,0},{48,16},{1,33},{17,49},{33,1},{49,17},{2,34}... | collective-permute-start | bytes 1769480 | tf_op jit(solution)/shard_map/ppermute | solution.py:27
  176.1 11.0 %collective-permute-start.14 = (bf16[384,512]{1,0:T(8,128)(2,1)S(1)}, bf16[384,512]{1,0:T(8,128)(2,1)S(1)}, u32[]{:S(2)}, u32[]{:S(2)}) collective-permute-start(bf16[384,512]{1,0:T(8,128)(2,1)S(1)} %slice.179), channel_id=1, source_target_pairs={{0,32},{16,48},{32,0},{48,16},{1,33},{17,49},{33,1},{49,17},{2,34}... | collective-permute-start | bytes 1179656 | tf_op jit(solution)/shard_map/ppermute | solution.py:27
  187.2 1.1 copy-start.5
  188.3 1.2 copy-start.8
Sparse Core Ops, SparseCore 0:
  21.3 77.4 all-gather.1
  101.3 73.6 reduce-scatter.1

commit v4 on v3

--- a/solution.py
+++ b/solution.py
@@ -111,14 +111,15 @@
 def shards(pre_act, down_weight, grad_out):
     x, yl, yh, c = (lax.axis_index(n) for n in ("x", "yl", "yh", "c"))
     pre32 = pre_act.astype(f32)
-    hid = gelu_value(pre32).astype(bf16)
-    low, high = hid[:, :384], hid[:, 384:]
+    low, high = pre_act[:, :384], pre_act[:, 384:]
     keep, give = jnp.where(yl == 0, low, high), jnp.where(yl == 0, high, low)
     got_h = swap_y(give, 1)
 
     keep_w, give_w = split_columns(after(down_weight, give), yl)
     got_w = swap_y(give_w, 1)
-    hidden = lax.all_gather(jnp.concatenate([keep, after(got_h, keep_w)], axis=0), "z", axis=1, tiled=True)
+    hid = jnp.concatenate([keep, after(got_h, keep_w)], axis=0)
+    hid = gelu_value(hid.astype(f32)).astype(bf16)
+    hidden = lax.all_gather(hid, "z", axis=1, tiled=True)
     own = jnp.concatenate([keep_w, got_w], axis=0)
     near = near4(swap_x, after(own, got_h))
     weight = jnp.concatenate([own, near[0], *far4(swap_x, *near), near[1]], axis=0)
@@ -132,11 +133,7 @@
     grads = table[(place & 1) * 4 + (place >> 1) * 2 + (yl ^ (iota & 1))].reshape(768, 1024)
 
     gh = lax.dot_general(weight, grads, (((0,), (0,)), ((), ())), preferred_element_type=f32).astype(bf16)
-    gh = lax.psum_scatter(after(gh, hidden), "z", scatter_dimension=0, tiled=True)
-    theirs = swap_y(gh[:, 512:], 1)
-    grad_hidden = join_columns(gh[:, :512].T, theirs.T, yl)
-    grad_pre = (grad_hidden.astype(f32) * gelu_slope(pre32)).astype(bf16)
-
+    gh = lax.psum_scatter(gh, "z", scatter_dimension=0, tiled=True)
     gw_all = jnp.dot(grads, hidden, preferred_element_type=f32).astype(bf16)
     gw = gw_all.reshape(4, 192, 3072)
     far = scatter_far(swap_x, gw[2])
@@ -148,7 +145,11 @@
     part = add(out[order[:4]], swap_c(out[order[4:]])).reshape(2, 192, 1024)
     output = scatter4(swap_y, [part[m >> 1, :, (m & 1) * 512 : (m & 1) * 512 + 512] for m in range(4)])
     total = add3(after(gw[0], output), *near).astype(bf16)
-    grad_weight = join_columns(after(total[:96], theirs), swap_y(total[96:], 1), yl)
+    got_gw = swap_y(total[96:], 1)
+    theirs = swap_y(after(gh, got_gw)[:, 512:], 1)
+    grad_hidden = join_columns(gh[:, :512].T, theirs.T, yl)
+    grad_pre = (grad_hidden.astype(f32) * gelu_slope(pre32)).astype(bf16)
+    grad_weight = join_columns(total[:96], got_gw, yl)
     output = output.T
     return output, grad_pre, grad_weight
 

time: 198 us -> 197 us (level)
  local copies, waits for them, and re-layouts: 14.7 us -> 10.4 us
  other arithmetic: 13.1 us -> 16.1 us
    reduce_scatter x1, waiting for transfers between devices: 12.4 us -> 0.02 us  [shards(): gh = lax.psum_scatter(gh, 'z', scatter_dimension=0, tiled=True)]
    ppermute x10, waiting for transfers between devices: 39.3 us -> 48.4 us  [swap_y(): return lax.ppermute(a, ('yl', 'yh'), [(i, i ^ flip) for i in range(4)])]
    ppermute x8, waiting for transfers between devices: 43.8 us -> 46.4 us  [swap_x(): return lax.ppermute(a, 'x', [(i, i ^ mask) for i in range(4)])]
    unnamed x44 -> x38, local copies, waits for them, and re-layouts: 8.16 us -> 6.01 us
  transfers between devices with their start and end apart: 22 -> 22, of which waited for: 16 -> 16; matrix products, arithmetic and copies ran while one was open for 22% -> 20% of each run, Pallas kernels for 1% -> 1%
where the time goes in v4:
time: 197 us
  waiting for transfers between devices  101 us (51%)
  starting transfers between devices  27.9 us (14%)
  matrix products  24.5 us (12%)
  other arithmetic  16.1 us (8%)
  between operations  14.5 us (7%)
  local copies, waits for them, and re-layouts  10.4 us (5%)
  Pallas kernels  2.4 us (1%)
    ppermute x10, waiting for transfers between devices, swap_y(): return lax.ppermute(a, ('yl', 'yh'), [(i, i ^ flip) for i in range(4)])  48.4 us
    ppermute x8, waiting for transfers between devices, swap_x(): return lax.ppermute(a, 'x', [(i, i ^ mask) for i in range(4)])  46.4 us
    ppermute x10, starting transfers between devices, swap_y(): return lax.ppermute(a, ('yl', 'yh'), [(i, i ^ flip) for i in range(4)])  14.8 us
    ppermute x8, starting transfers between devices, swap_x(): return lax.ppermute(a, 'x', [(i, i ^ mask) for i in range(4)])  12.6 us
    dot_general x1, matrix products, shards(): lax.dot_general(weight, grads, (((0,), (0,)), ((), ())), preferred_elemen...  9.42 us
    dot_general x1, matrix products, shards(): gw_all = jnp.dot(grads, hidden, preferred_element_type=f32).astype(bf16)  8.16 us
    dot_general x1, matrix products, shards(): lax.dot_general(weight, after(hidden, gw_all), (((1,), (1,)), ((), ())),...  6.95 us
    all_gather x1, waiting for transfers between devices, shards(): hidden = lax.all_gather(hid, 'z', axis=1, tiled=True)  6.23 us
  transfers between devices with their start and end apart: 22, of which 16 were waited for; matrix products, arithmetic and copies ran while one was open for 20% of the time, Pallas kernels for 1%

profile of v4, /device:TPU:2, one launch (start us, length us, event | category | flops | bytes accessed | tf_op | source)
XLA Modules:
  0.0 196.9 jit_solution(7081112717981679989)
XLA Ops:
  7.2 1.2 broadcast_select_fusion.2
  8.4 1.7 collective-permute-start.1
  10.1 2.4 %shard_map.58 = (bf16[96,3072]{1,0:T(8,128)(2,1)}, bf16[96,3072]{1,0:T(8,128)(2,1)}) custom-call(s32[1]{0:T(128)} %bitcast.which_ref, bf16[96,6144]{1,0:T(8,128)(2,1)} %a_ref), custom_call_target="tpu_custom_call" | custom-call | bytes 2359296 | tf_op jit(solution)/shard_map/pallas_call | solution.py:95
  12.5 6.9 %collective-permute-done.1 = bf16[512,384]{1,0:T(8,128)(2,1)S(1)} collective-permute-done((bf16[512,384]{1,0:T(8,128)(2,1)S(1)}, bf16[512,384]{1,0:T(8,128)(2,1)S(1)}, u32[]{:S(2)}, u32[]{:S(2)}) %collective-permute-start.1) | collective-permute-done | bytes 393248 | tf_op jit(solution)/shard_map/ppermute | solution.py:27
  19.4 1.4 fusion.1
  20.9 1.7 collective-permute-start
  22.5 12.6 %collective-permute-done = bf16[96,3072]{1,0:T(8,128)(2,1)S(1)} collective-permute-done((bf16[96,3072]{1,0:T(8,128)(2,1)S(1)}, bf16[96,3072]{1,0:T(8,128)(2,1)S(1)}, u32[]{:S(2)}, u32[]{:S(2)}) %collective-permute-start) | collective-permute-done | bytes 589856 | tf_op jit(solution)/shard_map/ppermute | solution.py:27
  35.2 1.1 pad_maximum_fusion.1
  36.2 0.2 collective-permute-start.2
  36.4 2.5 %collective-permute-start.4 = (bf16[192,3072]{1,0:T(8,128)(2,1)}, bf16[192,3072]{1,0:T(8,128)(2,1)S(1)}, u32[]{:S(2)}, u32[]{:S(2)}) collective-permute-start(bf16[192,3072]{1,0:T(8,128)(2,1)} %pad_maximum_fusion.1), channel_id=1, source_target_pairs={{0,192},{64,128},{128,64},{192,0},{1,193},{65,129},{129,65},{193,1... | collective-permute-start | bytes 3538952 | tf_op jit(solution)/shard_map/ppermute | solution.py:31
  39.1 23.3 %collective-permute-done.2 = bf16[192,3072]{1,0:T(8,128)(2,1)S(1)} collective-permute-done((bf16[192,3072]{1,0:T(8,128)(2,1)}, bf16[192,3072]{1,0:T(8,128)(2,1)S(1)}, u32[]{:S(2)}, u32[]{:S(2)}) %collective-permute-start.2) | collective-permute-done | bytes 1179680 | tf_op jit(solution)/shard_map/ppermute | solution.py:31
  62.4 3.0 %collective-permute-start.8 = (bf16[192,512]{1,0:T(8,128)(2,1)S(1)}, bf16[192,512]{1,0:T(8,128)(2,1)S(1)}, u32[]{:S(2)}, u32[]{:S(2)}) collective-permute-start(bf16[192,512]{1,0:T(8,128)(2,1)S(1)} %bitcast.41), channel_id=1, source_target_pairs={{0,48},{16,32},{32,16},{48,0},{1,49},{17,33},{33,17},{49,1},{2,50}... | collective-permute-start | bytes 589832 | tf_op jit(solution)/shard_map/ppermute | solution.py:27
  65.4 0.6 collective-permute-start.7
  66.0 0.5 collective-permute-start.6
  66.5 1.6 collective-permute-start.3
  68.1 1.9 collective-permute-start.5
  70.0 0.1 constant_dynamic-update-slice_fusion.3
  70.1 2.4 %collective-permute-done.6 = bf16[192,512]{1,0:T(8,128)(2,1)S(1)} collective-permute-done((bf16[192,512]{1,0:T(8,128)(2,1)S(1)}, bf16[192,512]{1,0:T(8,128)(2,1)S(1)}, u32[]{:S(2)}, u32[]{:S(2)}) %collective-permute-start.6) | collective-permute-done | bytes 196640 | tf_op jit(solution)/shard_map/ppermute | solution.py:27
  72.6 0.1 collective-permute-done.7
  72.9 0.3 collective-permute-start.9
  73.2 5.1 %collective-permute-done.3 = bf16[96,3072]{1,0:T(8,128)(2,1)S(1)} collective-permute-done((bf16[96,3072]{1,0:T(8,128)(2,1)S(1)}, bf16[96,3072]{1,0:T(8,128)(2,1)S(1)}, u32[]{:S(2)}, u32[]{:S(2)}) %collective-permute-start.3) | collective-permute-done | bytes 589856 | tf_op jit(solution)/shard_map/ppermute | solution.py:31
  78.3 1.4 collective-permute-done.5
  79.7 0.1 constant_dynamic-update-slice_fusion
  79.8 0.2 pad_maximum_fusion
  80.0 2.0 %copy-done.4 = bf16[768,3072]{1,0:T(8,128)(2,1)} copy-done((bf16[768,3072]{1,0:T(8,128)(2,1)}, bf16[768,3072]{1,0:T(8,128)(2,1)S(1)}, u32[]{:S(2)}) %copy-start.4) | copy-done | bytes 4718616
  82.0 0.6 gather_fusion
  82.6 9.4 %convolution_convert_fusion = bf16[3072,1024]{1,0:T(8,128)(2,1)} fusion(bf16[768,3072]{1,0:T(8,128)(2,1)} %copy-done.4, bf16[768,1024]{1,0:T(8,128)(2,1)S(1)} %bitcast.39), kind=kOutput, calls=%fused_computation.3 | convolution fusion | flops 4834983936 | bytes 12582912 | tf_op jit(solution)/shard_map/dot_general | solution.py:135
  92.2 6.2 %all-gather.2.cloned.1.call-done = bf16[1024,3072]{1,0:T(8,128)(2,1)} async-done(((bf16[1024,384]{1,0:T(8,128)(2,1)}), bf16[1024,3072]{1,0:T(8,128)(2,1)}) %all-gather.2.cloned.1.call-update) | async-done | bytes 6291472 | tf_op jit(solution)/shard_map/all_gather | solution.py:122
  98.4 8.2 %convolution_convert_fusion.1 = bf16[768,3072]{1,0:T(8,128)(2,1)S(1)} fusion(bf16[768,1024]{1,0:T(8,128)(2,1)S(1)} %bitcast.40, bf16[1024,3072]{1,0:T(8,128)(2,1)} %all-gather.2.cloned.1.call-done), kind=kOutput, calls=%fused_computation.4 | convolution fusion | flops 4834197504 | bytes 12582912 | tf_op jit(solution)/shard_map/dot_general | solution.py:137
  106.6 1.3 fusion.24
  107.9 1.1 copy-done
  109.0 1.5 collective-permute-start.14
  110.5 1.8 collective-permute-start.16
  112.3 7.0 %convolution_convert_fusion.2 = bf16[768,1024]{1,0:T(8,128)(2,1)S(1)} fusion(bf16[768,3072]{1,0:T(8,128)(2,1)} %copy-done.4, bf16[1024,3072]{1,0:T(8,128)(2,1)S(1)} %copy-done.6), kind=kOutput, calls=%fused_computation.18 | convolution fusion | flops 4832624640 | bytes 12582912 | tf_op jit(solution)/shard_map/dot_general | solution.py:140
  119.2 0.6 gather_fusion.2
  119.8 0.1 collective-permute-start.10
  119.9 4.5 %collective-permute-done.14 = bf16[96,3072]{1,0:T(8,128)(2,1)} collective-permute-done((bf16[96,3072]{1,0:T(8,128)(2,1)}, bf16[96,3072]{1,0:T(8,128)(2,1)}, u32[]{:S(2)}, u32[]{:S(2)}) %collective-permute-start.14) | collective-permute-done | bytes 589856 | tf_op jit(solution)/shard_map/ppermute | solution.py:31
  124.4 1.2 collective-permute-done.16
  125.6 2.1 %add_convert_fusion.3 = (bf16[96,3072]{1,0:T(8,128)(2,1)S(1)}, bf16[96,3072]{1,0:T(8,128)(2,1)S(1)}) fusion(bf16[96,3072]{1,0:T(8,128)(2,1)} %collective-permute-done.14, bf16[768,3072]{1,0:T(8,128)(2,1)} %copy-done, bf16[96,3072]{1,0:T(8,128)(2,1)} %collective-permute-done.16), kind=kLoop, calls=%fused_computation.39 | loop fusion | flops 2359296 | bytes 3538944 | tf_op jit(solution)/shard_map/convert_element_type | solution.py:50
  127.7 1.1 pad_maximum_fusion.3
  128.8 0.5 collective-permute-start.17
  129.2 1.1 pad_maximum_fusion.2
  130.3 2.8 %collective-permute-start.15 = (bf16[192,3072]{1,0:T(8,128)(2,1)}, bf16[192,3072]{1,0:T(8,128)(2,1)}, u32[]{:S(2)}, u32[]{:S(2)}) collective-permute-start(bf16[192,3072]{1,0:T(8,128)(2,1)} %pad_maximum_fusion.2), channel_id=1, source_target_pairs={{0,64},{64,0},{128,192},{192,128},{1,65},{65,1},{129,193},{193,129... | collective-permute-start | bytes 3538952 | tf_op jit(solution)/shard_map/ppermute | solution.py:31
  133.1 0.6 gather_fusion.1
  133.7 1.4 add_convert_fusion.1
  135.2 3.1 %collective-permute-start.13 = (bf16[192,512]{1,0:T(8,128)(2,1)S(1)}, bf16[192,512]{1,0:T(8,128)(2,1)S(1)}, u32[]{:S(2)}, u32[]{:S(2)}) collective-permute-start(bf16[192,512]{1,0:T(8,128)(2,1)S(1)} %get-tuple-element.39), channel_id=1, source_target_pairs={{0,16},{16,0},{32,48},{48,32},{1,17},{17,1},{33,49},{49,33},{2,18}... | collective-permute-start | bytes 589832 | tf_op jit(solution)/shard_map/ppermute | solution.py:27
  138.3 1.1 collective-permute-start.12
  139.5 4.2 %collective-permute-done.13 = bf16[192,512]{1,0:T(8,128)(2,1)S(1)} collective-permute-done((bf16[192,512]{1,0:T(8,128)(2,1)S(1)}, bf16[192,512]{1,0:T(8,128)(2,1)S(1)}, u32[]{:S(2)}, u32[]{:S(2)}) %collective-permute-start.13) | collective-permute-done | bytes 196640 | tf_op jit(solution)/shard_map/ppermute | solution.py:27
  143.7 2.9 %collective-permute-done.12 = bf16[192,512]{1,0:T(8,128)(2,1)S(1)} collective-permute-done((bf16[192,512]{1,0:T(8,128)(2,1)S(1)}, bf16[192,512]{1,0:T(8,128)(2,1)S(1)}, u32[]{:S(2)}, u32[]{:S(2)}) %collective-permute-start.12) | collective-permute-done | bytes 196640 | tf_op jit(solution)/shard_map/ppermute | solution.py:27
  146.5 0.8 fusion.16
  147.3 8.3 %collective-permute-done.17 = bf16[192,3072]{1,0:T(8,128)(2,1)} collective-permute-done((bf16[192,3072]{1,0:T(8,128)(2,1)}, bf16[192,3072]{1,0:T(8,128)(2,1)}, u32[]{:S(2)}, u32[]{:S(2)}) %collective-permute-start.17) | collective-permute-done | bytes 1179680 | tf_op jit(solution)/shard_map/ppermute | solution.py:31
  155.6 2.6 %collective-permute-done.15 = bf16[192,3072]{1,0:T(8,128)(2,1)} collective-permute-done((bf16[192,3072]{1,0:T(8,128)(2,1)}, bf16[192,3072]{1,0:T(8,128)(2,1)}, u32[]{:S(2)}, u32[]{:S(2)}) %collective-permute-start.15) | collective-permute-done | bytes 1179680 | tf_op jit(solution)/shard_map/ppermute | solution.py:31
  158.2 2.2 %add_convert_fusion = bf16[192,3072]{1,0:T(8,128)(2,1)S(1)} fusion(bf16[192,3072]{1,0:T(8,128)(2,1)} %collective-permute-done.17, bf16[192,3072]{1,0:T(8,128)(2,1)} %collective-permute-done.15, bf16[192,3072]{1,0:T(8,128)(2,1)S(1)} %slice-done), kind=kLoop, calls=%fused_computation.17 | loop fusion | flops 3538944 | bytes 4718592 | tf_op jit(solution)/shard_map/convert_element_type | solution.py:147
  160.4 1.6 collective-permute-start.18
  162.0 0.3 copy.6
  162.3 11.5 %collective-permute-done.18 = bf16[96,3072]{1,0:T(8,128)(2,1)} collective-permute-done((bf16[96,3072]{1,0:T(8,128)(2,1)S(1)}, bf16[96,3072]{1,0:T(8,128)(2,1)}, u32[]{:S(2)}, u32[]{:S(2)}) %collective-permute-start.18) | collective-permute-done | bytes 589856 | tf_op jit(solution)/shard_map/ppermute | solution.py:27
  173.9 1.2 broadcast_select_fusion
  175.3 1.0 slice.146
  176.4 1.6 collective-permute-start.19
  178.0 1.0 copy-done.5
  179.0 7.7 %collective-permute-done.19 = bf16[384,512]{1,0:T(8,128)(2,1)S(1)} collective-permute-done((bf16[384,512]{1,0:T(8,128)(2,1)S(1)}, bf16[384,512]{1,0:T(8,128)(2,1)S(1)}, u32[]{:S(2)}, u32[]{:S(2)}) %collective-permute-start.19) | collective-permute-done | bytes 393248 | tf_op jit(solution)/shard_map/ppermute | solution.py:27
  186.7 1.1 select_bitcast_fusion.1
  187.8 1.1 fusion.12
  188.9 1.2 copy.7
  (59 shorter events, 1.0 us)
Async XLA Ops:
  7.2 91.2 %all-gather.2.cloned.1.call-start = ((), (), s32[]{:S(2)}) async-start(), calls=%async_computation.1 | async-start | bytes 7077888 | tf_op jit(solution)/shard_map/all_gather | solution.py:122
  8.4 10.9 %collective-permute-start.1 = (bf16[512,384]{1,0:T(8,128)(2,1)S(1)}, bf16[512,384]{1,0:T(8,128)(2,1)S(1)}, u32[]{:S(2)}, u32[]{:S(2)}) collective-permute-start(bf16[512,384]{1,0:T(8,128)(2,1)S(1)} %get-tuple-element.42), channel_id=1, source_target_pairs={{0,32},{16,48},{32,0},{48,16},{1,33},{17,49},{33,1},{49,17},{2,34}... | collective-permute-start | bytes 1179656 | tf_op jit(solution)/shard_map/ppermute | solution.py:27
  12.5 8.4 %copy-start.7 = (bf16[96,3072]{1,0:T(8,128)(2,1)S(1)}, bf16[96,3072]{1,0:T(8,128)(2,1)}, u32[]{:S(2)}) copy-start(bf16[96,3072]{1,0:T(8,128)(2,1)} %get-tuple-element.16) | copy-start | bytes 1769476
  12.5 22.7 %copy-start.2 = (bf16[96,3072]{1,0:T(8,128)(2,1)S(1)}, bf16[96,3072]{1,0:T(8,128)(2,1)}, u32[]{:S(2)}) copy-start(bf16[96,3072]{1,0:T(8,128)(2,1)} %get-tuple-element.15) | copy-start | bytes 1769476
  20.8 154.5 %reduce-scatter.2.cloned.1.call-start = ((), (), s32[]{:S(2)}) async-start(), calls=%async_computation.2 | async-start | bytes 7077888 | tf_op jit(solution)/shard_map/reduce_scatter | solution.py:136
  20.9 14.3 %collective-permute-start = (bf16[96,3072]{1,0:T(8,128)(2,1)S(1)}, bf16[96,3072]{1,0:T(8,128)(2,1)S(1)}, u32[]{:S(2)}, u32[]{:S(2)}) collective-permute-start(bf16[96,3072]{1,0:T(8,128)(2,1)S(1)} %copy-done.7), channel_id=1, source_target_pairs={{0,32},{16,48},{32,0},{48,16},{1,33},{17,49},{33,1},{49,17},{2,34}... | collective-permute-start | bytes 1769480 | tf_op jit(solution)/shard_map/ppermute | solution.py:27
  36.2 26.1 %collective-permute-start.2 = (bf16[192,3072]{1,0:T(8,128)(2,1)}, bf16[192,3072]{1,0:T(8,128)(2,1)S(1)}, u32[]{:S(2)}, u32[]{:S(2)}) collective-permute-start(bf16[192,3072]{1,0:T(8,128)(2,1)} %pad_maximum_fusion.1), channel_id=1, source_target_pairs={{0,64},{64,0},{128,192},{192,128},{1,65},{65,1},{129,193},{193,129... | collective-permute-start | bytes 3538952 | tf_op jit(solution)/shard_map/ppermute | solution.py:31
  36.4 31.7 %collective-permute-start.4 = (bf16[192,3072]{1,0:T(8,128)(2,1)}, bf16[192,3072]{1,0:T(8,128)(2,1)S(1)}, u32[]{:S(2)}, u32[]{:S(2)}) collective-permute-start(bf16[192,3072]{1,0:T(8,128)(2,1)} %pad_maximum_fusion.1), channel_id=1, source_target_pairs={{0,192},{64,128},{128,64},{192,0},{1,193},{65,129},{129,65},{193,1... | collective-permute-start | bytes 3538952 | tf_op jit(solution)/shard_map/ppermute | solution.py:31
  38.9 23.4 %copy-start.3 = (bf16[512,192]{0,1:T(8,128)(2,1)S(1)}, bf16[512,192]{0,1:T(8,128)(2,1)}, u32[]{:S(2)}) copy-start(bf16[512,192]{0,1:T(8,128)(2,1)} %param.5) | copy-start | bytes 589828
  62.4 10.2 %collective-permute-start.8 = (bf16[192,512]{1,0:T(8,128)(2,1)S(1)}, bf16[192,512]{1,0:T(8,128)(2,1)S(1)}, u32[]{:S(2)}, u32[]{:S(2)}) collective-permute-start(bf16[192,512]{1,0:T(8,128)(2,1)S(1)} %bitcast.41), channel_id=1, source_target_pairs={{0,48},{16,32},{32,16},{48,0},{1,49},{17,33},{33,17},{49,1},{2,50}... | collective-permute-start | bytes 589832 | tf_op jit(solution)/shard_map/ppermute | solution.py:27
  65.4 7.4 %collective-permute-start.7 = (bf16[192,512]{1,0:T(8,128)(2,1)S(1)}, bf16[192,512]{1,0:T(8,128)(2,1)S(1)}, u32[]{:S(2)}, u32[]{:S(2)}) collective-permute-start(bf16[192,512]{1,0:T(8,128)(2,1)S(1)} %bitcast.42), channel_id=1, source_target_pairs={{0,16},{16,0},{32,48},{48,32},{1,17},{17,1},{33,49},{49,33},{2,18}... | collective-permute-start | bytes 589832 | tf_op jit(solution)/shard_map/ppermute | solution.py:27
  66.0 6.5 %collective-permute-start.6 = (bf16[192,512]{1,0:T(8,128)(2,1)S(1)}, bf16[192,512]{1,0:T(8,128)(2,1)S(1)}, u32[]{:S(2)}, u32[]{:S(2)}) collective-permute-start(bf16[192,512]{1,0:T(8,128)(2,1)S(1)} %bitcast.43), channel_id=1, source_target_pairs={{0,32},{16,48},{32,0},{48,16},{1,33},{17,49},{33,1},{49,17},{2,34}... | collective-permute-start | bytes 589832 | tf_op jit(solution)/shard_map/ppermute | solution.py:27
  66.5 11.8 %collective-permute-start.3 = (bf16[96,3072]{1,0:T(8,128)(2,1)S(1)}, bf16[96,3072]{1,0:T(8,128)(2,1)S(1)}, u32[]{:S(2)}, u32[]{:S(2)}) collective-permute-start(bf16[96,3072]{1,0:T(8,128)(2,1)S(1)} %slice.170), channel_id=1, source_target_pairs={{0,192},{64,128},{128,64},{192,0},{1,193},{65,129},{129,65},{193,1... | collective-permute-start | bytes 1769480 | tf_op jit(solution)/shard_map/ppermute | solution.py:31
  68.1 11.5 %collective-permute-start.5 = (bf16[96,3072]{1,0:T(8,128)(2,1)S(1)}, bf16[96,3072]{1,0:T(8,128)(2,1)S(1)}, u32[]{:S(2)}, u32[]{:S(2)}) collective-permute-start(bf16[96,3072]{1,0:T(8,128)(2,1)S(1)} %slice.171), channel_id=1, source_target_pairs={{0,64},{64,0},{128,192},{192,128},{1,65},{65,1},{129,193},{193,129... | collective-permute-start | bytes 1769480 | tf_op jit(solution)/shard_map/ppermute | solution.py:31
  72.9 7.0 %collective-permute-start.9 = (bf16[2,192,1024]{2,1,0:T(8,128)(2,1)S(1)}, bf16[2,192,1024]{2,1,0:T(8,128)(2,1)S(1)}, u32[]{:S(2)}, u32[]{:S(2)}) collective-permute-start(bf16[2,192,1024]{2,1,0:T(8,128)(2,1)S(1)} %pad_maximum_fusion.4), channel_id=1, source_target_pairs={{0,8},{8,0},{1,9},{9,1},{2,10},{10,2},{3,11},{11,3},{4,12},{12,4},... | collective-permute-start | bytes 2359304 | tf_op jit(solution)/shard_map/ppermute | solution.py:35
  79.8 2.2 %copy-start.4 = (bf16[768,3072]{1,0:T(8,128)(2,1)}, bf16[768,3072]{1,0:T(8,128)(2,1)S(1)}, u32[]{:S(2)}) copy-start(bf16[768,3072]{1,0:T(8,128)(2,1)S(1)} %constant_dynamic-update-slice_fusion) | copy-start | bytes 14155780
  98.4 13.9 %copy-start.6 = (bf16[1024,3072]{1,0:T(8,128)(2,1)S(1)}, bf16[1024,3072]{1,0:T(8,128)(2,1)}, u32[]{:S(2)}) copy-start(bf16[1024,3072]{1,0:T(8,128)(2,1)} %all-gather.2.cloned.1.call-done) | copy-start | bytes 18874372
  106.6 2.4 %copy-start = (bf16[768,3072]{1,0:T(8,128)(2,1)}, bf16[768,3072]{1,0:T(8,128)(2,1)S(1)}, u32[]{:S(2)}) copy-start(bf16[768,3072]{1,0:T(8,128)(2,1)S(1)} %convolution_convert_fusion.1) | copy-start | bytes 14155780
  109.0 15.4 %collective-permute-start.14 = (bf16[96,3072]{1,0:T(8,128)(2,1)}, bf16[96,3072]{1,0:T(8,128)(2,1)}, u32[]{:S(2)}, u32[]{:S(2)}) collective-permute-start(bf16[96,3072]{1,0:T(8,128)(2,1)} %get-tuple-element.31), channel_id=1, source_target_pairs={{0,192},{64,128},{128,64},{192,0},{1,193},{65,129},{129,65},{193,1... | collective-permute-start | bytes 1769480 | tf_op jit(solution)/shard_map/ppermute | solution.py:31
  110.5 15.1 %collective-permute-start.16 = (bf16[96,3072]{1,0:T(8,128)(2,1)}, bf16[96,3072]{1,0:T(8,128)(2,1)}, u32[]{:S(2)}, u32[]{:S(2)}) collective-permute-start(bf16[96,3072]{1,0:T(8,128)(2,1)} %get-tuple-element.30), channel_id=1, source_target_pairs={{0,64},{64,0},{128,192},{192,128},{1,65},{65,1},{129,193},{193,129... | collective-permute-start | bytes 1769480 | tf_op jit(solution)/shard_map/ppermute | solution.py:31
  119.8 13.9 %collective-permute-start.10 = (bf16[4,96,1024]{2,1,0:T(8,128)(2,1)S(1)}, bf16[4,96,1024]{2,1,0:T(8,128)(2,1)}, u32[]{:S(2)}, u32[]{:S(2)}) collective-permute-start(bf16[4,96,1024]{2,1,0:T(8,128)(2,1)S(1)} %gather_fusion.2), channel_id=1, source_target_pairs={{0,8},{8,0},{1,9},{9,1},{2,10},{10,2},{3,11},{11,3},{4,12},{12,4},... | collective-permute-start | bytes 2359304 | tf_op jit(solution)/shard_map/ppermute | solution.py:35
  128.8 26.8 %collective-permute-start.17 = (bf16[192,3072]{1,0:T(8,128)(2,1)}, bf16[192,3072]{1,0:T(8,128)(2,1)}, u32[]{:S(2)}, u32[]{:S(2)}) collective-permute-start(bf16[192,3072]{1,0:T(8,128)(2,1)} %pad_maximum_fusion.3), channel_id=1, source_target_pairs={{0,192},{64,128},{128,64},{192,0},{1,193},{65,129},{129,65},{193,1... | collective-permute-start | bytes 3538952 | tf_op jit(solution)/shard_map/ppermute | solution.py:31
  130.3 27.8 %collective-permute-start.15 = (bf16[192,3072]{1,0:T(8,128)(2,1)}, bf16[192,3072]{1,0:T(8,128)(2,1)}, u32[]{:S(2)}, u32[]{:S(2)}) collective-permute-start(bf16[192,3072]{1,0:T(8,128)(2,1)} %pad_maximum_fusion.2), channel_id=1, source_target_pairs={{0,64},{64,0},{128,192},{192,128},{1,65},{65,1},{129,193},{193,129... | collective-permute-start | bytes 3538952 | tf_op jit(solution)/shard_map/ppermute | solution.py:31
  135.2 8.4 %collective-permute-start.13 = (bf16[192,512]{1,0:T(8,128)(2,1)S(1)}, bf16[192,512]{1,0:T(8,128)(2,1)S(1)}, u32[]{:S(2)}, u32[]{:S(2)}) collective-permute-start(bf16[192,512]{1,0:T(8,128)(2,1)S(1)} %get-tuple-element.39), channel_id=1, source_target_pairs={{0,16},{16,0},{32,48},{48,32},{1,17},{17,1},{33,49},{49,33},{2,18}... | collective-permute-start | bytes 589832 | tf_op jit(solution)/shard_map/ppermute | solution.py:27
  138.3 8.2 %collective-permute-start.12 = (bf16[192,512]{1,0:T(8,128)(2,1)S(1)}, bf16[192,512]{1,0:T(8,128)(2,1)S(1)}, u32[]{:S(2)}, u32[]{:S(2)}) collective-permute-start(bf16[192,512]{1,0:T(8,128)(2,1)S(1)} %get-tuple-element.40), channel_id=1, source_target_pairs={{0,48},{16,32},{32,16},{48,0},{1,49},{17,33},{33,17},{49,1},{2,50}... | collective-permute-start | bytes 589832 | tf_op jit(solution)/shard_map/ppermute | solution.py:27
  139.5 18.7 %slice-start = ((bf16[768,3072]{1,0:T(8,128)(2,1)}), bf16[192,3072]{1,0:T(8,128)(2,1)S(1)}, s32[]{:S(2)}) async-start(bf16[768,3072]{1,0:T(8,128)(2,1)} %copy-done), calls=%async_computation.3 | async-start | bytes 2359296 | tf_op jit(solution)/shard_map/slice | solution.py:147
  139.5 7.1 %collective-permute-start.11 = (bf16[192,512]{1,0:T(8,128)(2,1)S(1)}, bf16[192,512]{1,0:T(8,128)(2,1)S(1)}, u32[]{:S(2)}, u32[]{:S(2)}) collective-permute-start(bf16[192,512]{1,0:T(8,128)(2,1)S(1)} %get-tuple-element.38), channel_id=1, source_target_pairs={{0,32},{16,48},{32,0},{48,16},{1,33},{17,49},{33,1},{49,17},{2,34}... | collective-permute-start | bytes 589832 | tf_op jit(solution)/shard_map/ppermute | solution.py:27
  160.4 1.6 copy-start.1
  160.4 13.4 %collective-permute-start.18 = (bf16[96,3072]{1,0:T(8,128)(2,1)S(1)}, bf16[96,3072]{1,0:T(8,128)(2,1)}, u32[]{:S(2)}, u32[]{:S(2)}) collective-permute-start(bf16[96,3072]{1,0:T(8,128)(2,1)S(1)} %slice.184), channel_id=1, source_target_pairs={{0,32},{16,48},{32,0},{48,16},{1,33},{17,49},{33,1},{49,17},{2,34}... | collective-permute-start | bytes 1769480 | tf_op jit(solution)/shard_map/ppermute | solution.py:27
  176.4 10.3 %collective-permute-start.19 = (bf16[384,512]{1,0:T(8,128)(2,1)S(1)}, bf16[384,512]{1,0:T(8,128)(2,1)S(1)}, u32[]{:S(2)}, u32[]{:S(2)}) collective-permute-start(bf16[384,512]{1,0:T(8,128)(2,1)S(1)} %slice.146), channel_id=1, source_target_pairs={{0,32},{16,48},{32,0},{48,16},{1,33},{17,49},{33,1},{49,17},{2,34}... | collective-permute-start | bytes 1179656 | tf_op jit(solution)/shard_map/ppermute | solution.py:27
  178.0 1.0 copy-start.5
Sparse Core Ops, SparseCore 0:
  20.9 77.4 all-gather.1
  101.0 73.6 reduce-scatter.1

commit v5 on v4

--- a/solution.py
+++ b/solution.py
@@ -146,7 +146,7 @@
     output = scatter4(swap_y, [part[m >> 1, :, (m & 1) * 512 : (m & 1) * 512 + 512] for m in range(4)])
     total = add3(after(gw[0], output), *near).astype(bf16)
     got_gw = swap_y(total[96:], 1)
-    theirs = swap_y(after(gh, got_gw)[:, 512:], 1)
+    theirs = swap_y(after(gh[:, 512:], got_gw), 1)
     grad_hidden = join_columns(gh[:, :512].T, theirs.T, yl)
     grad_pre = (grad_hidden.astype(f32) * gelu_slope(pre32)).astype(bf16)
     grad_weight = join_columns(total[:96], got_gw, yl)

time: 197 us -> 197 us (level)
  no operation moved by 1% of the time
where the time goes in v5:
time: 197 us
  waiting for transfers between devices  101 us (51%)
  starting transfers between devices  27.9 us (14%)
  matrix products  24.5 us (12%)
  other arithmetic  16.1 us (8%)
  between operations  14.5 us (7%)
  local copies, waits for them, and re-layouts  10.4 us (5%)
  Pallas kernels  2.4 us (1%)
    ppermute x10, waiting for transfers between devices, swap_y(): return lax.ppermute(a, ('yl', 'yh'), [(i, i ^ flip) for i in range(4)])  48.4 us
    ppermute x8, waiting for transfers between devices, swap_x(): return lax.ppermute(a, 'x', [(i, i ^ mask) for i in range(4)])  46.4 us
    ppermute x10, starting transfers between devices, swap_y(): return lax.ppermute(a, ('yl', 'yh'), [(i, i ^ flip) for i in range(4)])  14.8 us
    ppermute x8, starting transfers between devices, swap_x(): return lax.ppermute(a, 'x', [(i, i ^ mask) for i in range(4)])  12.6 us
    dot_general x1, matrix products, shards(): lax.dot_general(weight, grads, (((0,), (0,)), ((), ())), preferred_elemen...  9.42 us
    dot_general x1, matrix products, shards(): gw_all = jnp.dot(grads, hidden, preferred_element_type=f32).astype(bf16)  8.16 us
    dot_general x1, matrix products, shards(): lax.dot_general(weight, after(hidden, gw_all), (((1,), (1,)), ((), ())),...  6.95 us
    all_gather x1, waiting for transfers between devices, shards(): hidden = lax.all_gather(hid, 'z', axis=1, tiled=True)  6.23 us
  transfers between devices with their start and end apart: 22, of which 16 were waited for; matrix products, arithmetic and copies ran while one was open for 20% of the time, Pallas kernels for 1%

profile of v5, /device:TPU:2, one launch (start us, length us, event | category | flops | bytes accessed | tf_op | source)
XLA Modules:
  0.0 196.9 jit_solution(7081112717981679989)
XLA Ops:
  7.2 1.2 broadcast_select_fusion.2
  8.4 1.7 collective-permute-start.1
  10.1 2.4 %shard_map.58 = (bf16[96,3072]{1,0:T(8,128)(2,1)}, bf16[96,3072]{1,0:T(8,128)(2,1)}) custom-call(s32[1]{0:T(128)} %bitcast.which_ref, bf16[96,6144]{1,0:T(8,128)(2,1)} %a_ref), custom_call_target="tpu_custom_call" | custom-call | bytes 2359296 | tf_op jit(solution)/shard_map/pallas_call | solution.py:95
  12.5 6.9 %collective-permute-done.1 = bf16[512,384]{1,0:T(8,128)(2,1)S(1)} collective-permute-done((bf16[512,384]{1,0:T(8,128)(2,1)S(1)}, bf16[512,384]{1,0:T(8,128)(2,1)S(1)}, u32[]{:S(2)}, u32[]{:S(2)}) %collective-permute-start.1) | collective-permute-done | bytes 393248 | tf_op jit(solution)/shard_map/ppermute | solution.py:27
  19.4 1.4 fusion.1
  20.9 1.7 collective-permute-start
  22.5 12.6 %collective-permute-done = bf16[96,3072]{1,0:T(8,128)(2,1)S(1)} collective-permute-done((bf16[96,3072]{1,0:T(8,128)(2,1)S(1)}, bf16[96,3072]{1,0:T(8,128)(2,1)S(1)}, u32[]{:S(2)}, u32[]{:S(2)}) %collective-permute-start) | collective-permute-done | bytes 589856 | tf_op jit(solution)/shard_map/ppermute | solution.py:27
  35.2 1.1 pad_maximum_fusion.1
  36.2 0.2 collective-permute-start.2
  36.4 2.5 %collective-permute-start.4 = (bf16[192,3072]{1,0:T(8,128)(2,1)}, bf16[192,3072]{1,0:T(8,128)(2,1)S(1)}, u32[]{:S(2)}, u32[]{:S(2)}) collective-permute-start(bf16[192,3072]{1,0:T(8,128)(2,1)} %pad_maximum_fusion.1), channel_id=1, source_target_pairs={{0,192},{64,128},{128,64},{192,0},{1,193},{65,129},{129,65},{193,1... | collective-permute-start | bytes 3538952 | tf_op jit(solution)/shard_map/ppermute | solution.py:31
  39.1 23.3 %collective-permute-done.2 = bf16[192,3072]{1,0:T(8,128)(2,1)S(1)} collective-permute-done((bf16[192,3072]{1,0:T(8,128)(2,1)}, bf16[192,3072]{1,0:T(8,128)(2,1)S(1)}, u32[]{:S(2)}, u32[]{:S(2)}) %collective-permute-start.2) | collective-permute-done | bytes 1179680 | tf_op jit(solution)/shard_map/ppermute | solution.py:31
  62.4 3.0 %collective-permute-start.8 = (bf16[192,512]{1,0:T(8,128)(2,1)S(1)}, bf16[192,512]{1,0:T(8,128)(2,1)S(1)}, u32[]{:S(2)}, u32[]{:S(2)}) collective-permute-start(bf16[192,512]{1,0:T(8,128)(2,1)S(1)} %bitcast.41), channel_id=1, source_target_pairs={{0,48},{16,32},{32,16},{48,0},{1,49},{17,33},{33,17},{49,1},{2,50}... | collective-permute-start | bytes 589832 | tf_op jit(solution)/shard_map/ppermute | solution.py:27
  65.4 0.6 collective-permute-start.7
  66.0 0.5 collective-permute-start.6
  66.5 1.6 collective-permute-start.3
  68.1 1.9 collective-permute-start.5
  70.0 0.1 constant_dynamic-update-slice_fusion.3
  70.1 2.4 %collective-permute-done.6 = bf16[192,512]{1,0:T(8,128)(2,1)S(1)} collective-permute-done((bf16[192,512]{1,0:T(8,128)(2,1)S(1)}, bf16[192,512]{1,0:T(8,128)(2,1)S(1)}, u32[]{:S(2)}, u32[]{:S(2)}) %collective-permute-start.6) | collective-permute-done | bytes 196640 | tf_op jit(solution)/shard_map/ppermute | solution.py:27
  72.6 0.1 collective-permute-done.7
  72.9 0.3 collective-permute-start.9
  73.2 5.1 %collective-permute-done.3 = bf16[96,3072]{1,0:T(8,128)(2,1)S(1)} collective-permute-done((bf16[96,3072]{1,0:T(8,128)(2,1)S(1)}, bf16[96,3072]{1,0:T(8,128)(2,1)S(1)}, u32[]{:S(2)}, u32[]{:S(2)}) %collective-permute-start.3) | collective-permute-done | bytes 589856 | tf_op jit(solution)/shard_map/ppermute | solution.py:31
  78.3 1.4 collective-permute-done.5
  79.7 0.1 constant_dynamic-update-slice_fusion
  79.8 0.2 pad_maximum_fusion
  80.0 2.0 %copy-done.4 = bf16[768,3072]{1,0:T(8,128)(2,1)} copy-done((bf16[768,3072]{1,0:T(8,128)(2,1)}, bf16[768,3072]{1,0:T(8,128)(2,1)S(1)}, u32[]{:S(2)}) %copy-start.4) | copy-done | bytes 4718616
  82.0 0.6 gather_fusion
  82.6 9.4 %convolution_convert_fusion = bf16[3072,1024]{1,0:T(8,128)(2,1)} fusion(bf16[768,3072]{1,0:T(8,128)(2,1)} %copy-done.4, bf16[768,1024]{1,0:T(8,128)(2,1)S(1)} %bitcast.39), kind=kOutput, calls=%fused_computation.3 | convolution fusion | flops 4834983936 | bytes 12582912 | tf_op jit(solution)/shard_map/dot_general | solution.py:135
  92.2 6.2 %all-gather.2.cloned.1.call-done = bf16[1024,3072]{1,0:T(8,128)(2,1)} async-done(((bf16[1024,384]{1,0:T(8,128)(2,1)}), bf16[1024,3072]{1,0:T(8,128)(2,1)}) %all-gather.2.cloned.1.call-update) | async-done | bytes 6291472 | tf_op jit(solution)/shard_map/all_gather | solution.py:122
  98.4 8.2 %convolution_convert_fusion.1 = bf16[768,3072]{1,0:T(8,128)(2,1)S(1)} fusion(bf16[768,1024]{1,0:T(8,128)(2,1)S(1)} %bitcast.40, bf16[1024,3072]{1,0:T(8,128)(2,1)} %all-gather.2.cloned.1.call-done), kind=kOutput, calls=%fused_computation.4 | convolution fusion | flops 4834197504 | bytes 12582912 | tf_op jit(solution)/shard_map/dot_general | solution.py:137
  106.6 1.3 fusion.24
  107.9 1.1 copy-done
  109.0 1.5 collective-permute-start.14
  110.5 1.8 collective-permute-start.16
  112.3 7.0 %convolution_convert_fusion.2 = bf16[768,1024]{1,0:T(8,128)(2,1)S(1)} fusion(bf16[768,3072]{1,0:T(8,128)(2,1)} %copy-done.4, bf16[1024,3072]{1,0:T(8,128)(2,1)S(1)} %copy-done.6), kind=kOutput, calls=%fused_computation.18 | convolution fusion | flops 4832624640 | bytes 12582912 | tf_op jit(solution)/shard_map/dot_general | solution.py:140
  119.2 0.6 gather_fusion.2
  119.8 0.1 collective-permute-start.10
  119.9 4.5 %collective-permute-done.14 = bf16[96,3072]{1,0:T(8,128)(2,1)} collective-permute-done((bf16[96,3072]{1,0:T(8,128)(2,1)}, bf16[96,3072]{1,0:T(8,128)(2,1)}, u32[]{:S(2)}, u32[]{:S(2)}) %collective-permute-start.14) | collective-permute-done | bytes 589856 | tf_op jit(solution)/shard_map/ppermute | solution.py:31
  124.4 1.2 collective-permute-done.16
  125.6 2.1 %add_convert_fusion.3 = (bf16[96,3072]{1,0:T(8,128)(2,1)S(1)}, bf16[96,3072]{1,0:T(8,128)(2,1)S(1)}) fusion(bf16[96,3072]{1,0:T(8,128)(2,1)} %collective-permute-done.14, bf16[768,3072]{1,0:T(8,128)(2,1)} %copy-done, bf16[96,3072]{1,0:T(8,128)(2,1)} %collective-permute-done.16), kind=kLoop, calls=%fused_computation.39 | loop fusion | flops 2359296 | bytes 3538944 | tf_op jit(solution)/shard_map/convert_element_type | solution.py:50
  127.7 1.1 pad_maximum_fusion.3
  128.8 0.5 collective-permute-start.17
  129.2 1.1 pad_maximum_fusion.2
  130.3 2.8 %collective-permute-start.15 = (bf16[192,3072]{1,0:T(8,128)(2,1)}, bf16[192,3072]{1,0:T(8,128)(2,1)}, u32[]{:S(2)}, u32[]{:S(2)}) collective-permute-start(bf16[192,3072]{1,0:T(8,128)(2,1)} %pad_maximum_fusion.2), channel_id=1, source_target_pairs={{0,64},{64,0},{128,192},{192,128},{1,65},{65,1},{129,193},{193,129... | collective-permute-start | bytes 3538952 | tf_op jit(solution)/shard_map/ppermute | solution.py:31
  133.1 0.6 gather_fusion.1
  133.7 1.4 add_convert_fusion.1
  135.2 3.1 %collective-permute-start.13 = (bf16[192,512]{1,0:T(8,128)(2,1)S(1)}, bf16[192,512]{1,0:T(8,128)(2,1)S(1)}, u32[]{:S(2)}, u32[]{:S(2)}) collective-permute-start(bf16[192,512]{1,0:T(8,128)(2,1)S(1)} %get-tuple-element.39), channel_id=1, source_target_pairs={{0,16},{16,0},{32,48},{48,32},{1,17},{17,1},{33,49},{49,33},{2,18}... | collective-permute-start | bytes 589832 | tf_op jit(solution)/shard_map/ppermute | solution.py:27
  138.3 1.1 collective-permute-start.12
  139.5 4.2 %collective-permute-done.13 = bf16[192,512]{1,0:T(8,128)(2,1)S(1)} collective-permute-done((bf16[192,512]{1,0:T(8,128)(2,1)S(1)}, bf16[192,512]{1,0:T(8,128)(2,1)S(1)}, u32[]{:S(2)}, u32[]{:S(2)}) %collective-permute-start.13) | collective-permute-done | bytes 196640 | tf_op jit(solution)/shard_map/ppermute | solution.py:27
  143.7 2.9 %collective-permute-done.12 = bf16[192,512]{1,0:T(8,128)(2,1)S(1)} collective-permute-done((bf16[192,512]{1,0:T(8,128)(2,1)S(1)}, bf16[192,512]{1,0:T(8,128)(2,1)S(1)}, u32[]{:S(2)}, u32[]{:S(2)}) %collective-permute-start.12) | collective-permute-done | bytes 196640 | tf_op jit(solution)/shard_map/ppermute | solution.py:27
  146.5 0.8 fusion.16
  147.3 8.3 %collective-permute-done.17 = bf16[192,3072]{1,0:T(8,128)(2,1)} collective-permute-done((bf16[192,3072]{1,0:T(8,128)(2,1)}, bf16[192,3072]{1,0:T(8,128)(2,1)}, u32[]{:S(2)}, u32[]{:S(2)}) %collective-permute-start.17) | collective-permute-done | bytes 1179680 | tf_op jit(solution)/shard_map/ppermute | solution.py:31
  155.6 2.6 %collective-permute-done.15 = bf16[192,3072]{1,0:T(8,128)(2,1)} collective-permute-done((bf16[192,3072]{1,0:T(8,128)(2,1)}, bf16[192,3072]{1,0:T(8,128)(2,1)}, u32[]{:S(2)}, u32[]{:S(2)}) %collective-permute-start.15) | collective-permute-done | bytes 1179680 | tf_op jit(solution)/shard_map/ppermute | solution.py:31
  158.2 2.2 %add_convert_fusion = bf16[192,3072]{1,0:T(8,128)(2,1)S(1)} fusion(bf16[192,3072]{1,0:T(8,128)(2,1)} %collective-permute-done.17, bf16[192,3072]{1,0:T(8,128)(2,1)} %collective-permute-done.15, bf16[192,3072]{1,0:T(8,128)(2,1)S(1)} %slice-done), kind=kLoop, calls=%fused_computation.17 | loop fusion | flops 3538944 | bytes 4718592 | tf_op jit(solution)/shard_map/convert_element_type | solution.py:147
  160.4 1.6 collective-permute-start.18
  162.0 0.3 copy.6
  162.3 11.5 %collective-permute-done.18 = bf16[96,3072]{1,0:T(8,128)(2,1)} collective-permute-done((bf16[96,3072]{1,0:T(8,128)(2,1)S(1)}, bf16[96,3072]{1,0:T(8,128)(2,1)}, u32[]{:S(2)}, u32[]{:S(2)}) %collective-permute-start.18) | collective-permute-done | bytes 589856 | tf_op jit(solution)/shard_map/ppermute | solution.py:27
  173.9 1.2 broadcast_select_fusion
  175.3 1.0 slice.177
  176.4 1.6 collective-permute-start.19
  178.0 1.0 copy-done.5
  179.0 7.7 %collective-permute-done.19 = bf16[384,512]{1,0:T(8,128)(2,1)S(1)} collective-permute-done((bf16[384,512]{1,0:T(8,128)(2,1)S(1)}, bf16[384,512]{1,0:T(8,128)(2,1)S(1)}, u32[]{:S(2)}, u32[]{:S(2)}) %collective-permute-start.19) | collective-permute-done | bytes 393248 | tf_op jit(solution)/shard_map/ppermute | solution.py:27
  186.7 1.1 select_bitcast_fusion.1
  187.8 1.1 fusion.12
  188.9 1.2 copy.7
  (59 shorter events, 1.0 us)
Async XLA Ops:
  7.2 91.2 %all-gather.2.cloned.1.call-start = ((), (), s32[]{:S(2)}) async-start(), calls=%async_computation.1 | async-start | bytes 7077888 | tf_op jit(solution)/shard_map/all_gather | solution.py:122
  8.4 10.9 %collective-permute-start.1 = (bf16[512,384]{1,0:T(8,128)(2,1)S(1)}, bf16[512,384]{1,0:T(8,128)(2,1)S(1)}, u32[]{:S(2)}, u32[]{:S(2)}) collective-permute-start(bf16[512,384]{1,0:T(8,128)(2,1)S(1)} %get-tuple-element.42), channel_id=1, source_target_pairs={{0,32},{16,48},{32,0},{48,16},{1,33},{17,49},{33,1},{49,17},{2,34}... | collective-permute-start | bytes 1179656 | tf_op jit(solution)/shard_map/ppermute | solution.py:27
  12.5 8.4 %copy-start.7 = (bf16[96,3072]{1,0:T(8,128)(2,1)S(1)}, bf16[96,3072]{1,0:T(8,128)(2,1)}, u32[]{:S(2)}) copy-start(bf16[96,3072]{1,0:T(8,128)(2,1)} %get-tuple-element.16) | copy-start | bytes 1769476
  12.5 22.7 %copy-start.2 = (bf16[96,3072]{1,0:T(8,128)(2,1)S(1)}, bf16[96,3072]{1,0:T(8,128)(2,1)}, u32[]{:S(2)}) copy-start(bf16[96,3072]{1,0:T(8,128)(2,1)} %get-tuple-element.15) | copy-start | bytes 1769476
  20.8 154.5 %reduce-scatter.2.cloned.1.call-start = ((), (), s32[]{:S(2)}) async-start(), calls=%async_computation.2 | async-start | bytes 7077888 | tf_op jit(solution)/shard_map/reduce_scatter | solution.py:136
  20.9 14.3 %collective-permute-start = (bf16[96,3072]{1,0:T(8,128)(2,1)S(1)}, bf16[96,3072]{1,0:T(8,128)(2,1)S(1)}, u32[]{:S(2)}, u32[]{:S(2)}) collective-permute-start(bf16[96,3072]{1,0:T(8,128)(2,1)S(1)} %copy-done.7), channel_id=1, source_target_pairs={{0,32},{16,48},{32,0},{48,16},{1,33},{17,49},{33,1},{49,17},{2,34}... | collective-permute-start | bytes 1769480 | tf_op jit(solution)/shard_map/ppermute | solution.py:27
  36.2 26.1 %collective-permute-start.2 = (bf16[192,3072]{1,0:T(8,128)(2,1)}, bf16[192,3072]{1,0:T(8,128)(2,1)S(1)}, u32[]{:S(2)}, u32[]{:S(2)}) collective-permute-start(bf16[192,3072]{1,0:T(8,128)(2,1)} %pad_maximum_fusion.1), channel_id=1, source_target_pairs={{0,64},{64,0},{128,192},{192,128},{1,65},{65,1},{129,193},{193,129... | collective-permute-start | bytes 3538952 | tf_op jit(solution)/shard_map/ppermute | solution.py:31
  36.4 31.7 %collective-permute-start.4 = (bf16[192,3072]{1,0:T(8,128)(2,1)}, bf16[192,3072]{1,0:T(8,128)(2,1)S(1)}, u32[]{:S(2)}, u32[]{:S(2)}) collective-permute-start(bf16[192,3072]{1,0:T(8,128)(2,1)} %pad_maximum_fusion.1), channel_id=1, source_target_pairs={{0,192},{64,128},{128,64},{192,0},{1,193},{65,129},{129,65},{193,1... | collective-permute-start | bytes 3538952 | tf_op jit(solution)/shard_map/ppermute | solution.py:31
  38.9 23.4 %copy-start.3 = (bf16[512,192]{0,1:T(8,128)(2,1)S(1)}, bf16[512,192]{0,1:T(8,128)(2,1)}, u32[]{:S(2)}) copy-start(bf16[512,192]{0,1:T(8,128)(2,1)} %param.5) | copy-start | bytes 589828
  62.4 10.2 %collective-permute-start.8 = (bf16[192,512]{1,0:T(8,128)(2,1)S(1)}, bf16[192,512]{1,0:T(8,128)(2,1)S(1)}, u32[]{:S(2)}, u32[]{:S(2)}) collective-permute-start(bf16[192,512]{1,0:T(8,128)(2,1)S(1)} %bitcast.41), channel_id=1, source_target_pairs={{0,48},{16,32},{32,16},{48,0},{1,49},{17,33},{33,17},{49,1},{2,50}... | collective-permute-start | bytes 589832 | tf_op jit(solution)/shard_map/ppermute | solution.py:27
  65.4 7.4 %collective-permute-start.7 = (bf16[192,512]{1,0:T(8,128)(2,1)S(1)}, bf16[192,512]{1,0:T(8,128)(2,1)S(1)}, u32[]{:S(2)}, u32[]{:S(2)}) collective-permute-start(bf16[192,512]{1,0:T(8,128)(2,1)S(1)} %bitcast.42), channel_id=1, source_target_pairs={{0,16},{16,0},{32,48},{48,32},{1,17},{17,1},{33,49},{49,33},{2,18}... | collective-permute-start | bytes 589832 | tf_op jit(solution)/shard_map/ppermute | solution.py:27
  66.0 6.5 %collective-permute-start.6 = (bf16[192,512]{1,0:T(8,128)(2,1)S(1)}, bf16[192,512]{1,0:T(8,128)(2,1)S(1)}, u32[]{:S(2)}, u32[]{:S(2)}) collective-permute-start(bf16[192,512]{1,0:T(8,128)(2,1)S(1)} %bitcast.43), channel_id=1, source_target_pairs={{0,32},{16,48},{32,0},{48,16},{1,33},{17,49},{33,1},{49,17},{2,34}... | collective-permute-start | bytes 589832 | tf_op jit(solution)/shard_map/ppermute | solution.py:27
  66.5 11.8 %collective-permute-start.3 = (bf16[96,3072]{1,0:T(8,128)(2,1)S(1)}, bf16[96,3072]{1,0:T(8,128)(2,1)S(1)}, u32[]{:S(2)}, u32[]{:S(2)}) collective-permute-start(bf16[96,3072]{1,0:T(8,128)(2,1)S(1)} %slice.170), channel_id=1, source_target_pairs={{0,192},{64,128},{128,64},{192,0},{1,193},{65,129},{129,65},{193,1... | collective-permute-start | bytes 1769480 | tf_op jit(solution)/shard_map/ppermute | solution.py:31
  68.1 11.5 %collective-permute-start.5 = (bf16[96,3072]{1,0:T(8,128)(2,1)S(1)}, bf16[96,3072]{1,0:T(8,128)(2,1)S(1)}, u32[]{:S(2)}, u32[]{:S(2)}) collective-permute-start(bf16[96,3072]{1,0:T(8,128)(2,1)S(1)} %slice.171), channel_id=1, source_target_pairs={{0,64},{64,0},{128,192},{192,128},{1,65},{65,1},{129,193},{193,129... | collective-permute-start | bytes 1769480 | tf_op jit(solution)/shard_map/ppermute | solution.py:31
  72.9 7.0 %collective-permute-start.9 = (bf16[2,192,1024]{2,1,0:T(8,128)(2,1)S(1)}, bf16[2,192,1024]{2,1,0:T(8,128)(2,1)S(1)}, u32[]{:S(2)}, u32[]{:S(2)}) collective-permute-start(bf16[2,192,1024]{2,1,0:T(8,128)(2,1)S(1)} %pad_maximum_fusion.4), channel_id=1, source_target_pairs={{0,8},{8,0},{1,9},{9,1},{2,10},{10,2},{3,11},{11,3},{4,12},{12,4},... | collective-permute-start | bytes 2359304 | tf_op jit(solution)/shard_map/ppermute | solution.py:35
  79.8 2.2 %copy-start.4 = (bf16[768,3072]{1,0:T(8,128)(2,1)}, bf16[768,3072]{1,0:T(8,128)(2,1)S(1)}, u32[]{:S(2)}) copy-start(bf16[768,3072]{1,0:T(8,128)(2,1)S(1)} %constant_dynamic-update-slice_fusion) | copy-start | bytes 14155780
  98.4 13.9 %copy-start.6 = (bf16[1024,3072]{1,0:T(8,128)(2,1)S(1)}, bf16[1024,3072]{1,0:T(8,128)(2,1)}, u32[]{:S(2)}) copy-start(bf16[1024,3072]{1,0:T(8,128)(2,1)} %all-gather.2.cloned.1.call-done) | copy-start | bytes 18874372
  106.6 2.4 %copy-start = (bf16[768,3072]{1,0:T(8,128)(2,1)}, bf16[768,3072]{1,0:T(8,128)(2,1)S(1)}, u32[]{:S(2)}) copy-start(bf16[768,3072]{1,0:T(8,128)(2,1)S(1)} %convolution_convert_fusion.1) | copy-start | bytes 14155780
  109.0 15.4 %collective-permute-start.14 = (bf16[96,3072]{1,0:T(8,128)(2,1)}, bf16[96,3072]{1,0:T(8,128)(2,1)}, u32[]{:S(2)}, u32[]{:S(2)}) collective-permute-start(bf16[96,3072]{1,0:T(8,128)(2,1)} %get-tuple-element.31), channel_id=1, source_target_pairs={{0,192},{64,128},{128,64},{192,0},{1,193},{65,129},{129,65},{193,1... | collective-permute-start | bytes 1769480 | tf_op jit(solution)/shard_map/ppermute | solution.py:31
  110.5 15.1 %collective-permute-start.16 = (bf16[96,3072]{1,0:T(8,128)(2,1)}, bf16[96,3072]{1,0:T(8,128)(2,1)}, u32[]{:S(2)}, u32[]{:S(2)}) collective-permute-start(bf16[96,3072]{1,0:T(8,128)(2,1)} %get-tuple-element.30), channel_id=1, source_target_pairs={{0,64},{64,0},{128,192},{192,128},{1,65},{65,1},{129,193},{193,129... | collective-permute-start | bytes 1769480 | tf_op jit(solution)/shard_map/ppermute | solution.py:31
  119.8 13.9 %collective-permute-start.10 = (bf16[4,96,1024]{2,1,0:T(8,128)(2,1)S(1)}, bf16[4,96,1024]{2,1,0:T(8,128)(2,1)}, u32[]{:S(2)}, u32[]{:S(2)}) collective-permute-start(bf16[4,96,1024]{2,1,0:T(8,128)(2,1)S(1)} %gather_fusion.2), channel_id=1, source_target_pairs={{0,8},{8,0},{1,9},{9,1},{2,10},{10,2},{3,11},{11,3},{4,12},{12,4},... | collective-permute-start | bytes 2359304 | tf_op jit(solution)/shard_map/ppermute | solution.py:35
  128.8 26.8 %collective-permute-start.17 = (bf16[192,3072]{1,0:T(8,128)(2,1)}, bf16[192,3072]{1,0:T(8,128)(2,1)}, u32[]{:S(2)}, u32[]{:S(2)}) collective-permute-start(bf16[192,3072]{1,0:T(8,128)(2,1)} %pad_maximum_fusion.3), channel_id=1, source_target_pairs={{0,192},{64,128},{128,64},{192,0},{1,193},{65,129},{129,65},{193,1... | collective-permute-start | bytes 3538952 | tf_op jit(solution)/shard_map/ppermute | solution.py:31
  130.3 27.8 %collective-permute-start.15 = (bf16[192,3072]{1,0:T(8,128)(2,1)}, bf16[192,3072]{1,0:T(8,128)(2,1)}, u32[]{:S(2)}, u32[]{:S(2)}) collective-permute-start(bf16[192,3072]{1,0:T(8,128)(2,1)} %pad_maximum_fusion.2), channel_id=1, source_target_pairs={{0,64},{64,0},{128,192},{192,128},{1,65},{65,1},{129,193},{193,129... | collective-permute-start | bytes 3538952 | tf_op jit(solution)/shard_map/ppermute | solution.py:31
  135.2 8.4 %collective-permute-start.13 = (bf16[192,512]{1,0:T(8,128)(2,1)S(1)}, bf16[192,512]{1,0:T(8,128)(2,1)S(1)}, u32[]{:S(2)}, u32[]{:S(2)}) collective-permute-start(bf16[192,512]{1,0:T(8,128)(2,1)S(1)} %get-tuple-element.39), channel_id=1, source_target_pairs={{0,16},{16,0},{32,48},{48,32},{1,17},{17,1},{33,49},{49,33},{2,18}... | collective-permute-start | bytes 589832 | tf_op jit(solution)/shard_map/ppermute | solution.py:27
  138.3 8.2 %collective-permute-start.12 = (bf16[192,512]{1,0:T(8,128)(2,1)S(1)}, bf16[192,512]{1,0:T(8,128)(2,1)S(1)}, u32[]{:S(2)}, u32[]{:S(2)}) collective-permute-start(bf16[192,512]{1,0:T(8,128)(2,1)S(1)} %get-tuple-element.40), channel_id=1, source_target_pairs={{0,48},{16,32},{32,16},{48,0},{1,49},{17,33},{33,17},{49,1},{2,50}... | collective-permute-start | bytes 589832 | tf_op jit(solution)/shard_map/ppermute | solution.py:27
  139.5 18.7 %slice-start = ((bf16[768,3072]{1,0:T(8,128)(2,1)}), bf16[192,3072]{1,0:T(8,128)(2,1)S(1)}, s32[]{:S(2)}) async-start(bf16[768,3072]{1,0:T(8,128)(2,1)} %copy-done), calls=%async_computation.3 | async-start | bytes 2359296 | tf_op jit(solution)/shard_map/slice | solution.py:147
  139.5 7.1 %collective-permute-start.11 = (bf16[192,512]{1,0:T(8,128)(2,1)S(1)}, bf16[192,512]{1,0:T(8,128)(2,1)S(1)}, u32[]{:S(2)}, u32[]{:S(2)}) collective-permute-start(bf16[192,512]{1,0:T(8,128)(2,1)S(1)} %get-tuple-element.38), channel_id=1, source_target_pairs={{0,32},{16,48},{32,0},{48,16},{1,33},{17,49},{33,1},{49,17},{2,34}... | collective-permute-start | bytes 589832 | tf_op jit(solution)/shard_map/ppermute | solution.py:27
  160.4 1.6 copy-start.1
  160.4 13.4 %collective-permute-start.18 = (bf16[96,3072]{1,0:T(8,128)(2,1)S(1)}, bf16[96,3072]{1,0:T(8,128)(2,1)}, u32[]{:S(2)}, u32[]{:S(2)}) collective-permute-start(bf16[96,3072]{1,0:T(8,128)(2,1)S(1)} %slice.185), channel_id=1, source_target_pairs={{0,32},{16,48},{32,0},{48,16},{1,33},{17,49},{33,1},{49,17},{2,34}... | collective-permute-start | bytes 1769480 | tf_op jit(solution)/shard_map/ppermute | solution.py:27
  176.4 10.3 %collective-permute-start.19 = (bf16[384,512]{1,0:T(8,128)(2,1)S(1)}, bf16[384,512]{1,0:T(8,128)(2,1)S(1)}, u32[]{:S(2)}, u32[]{:S(2)}) collective-permute-start(bf16[384,512]{1,0:T(8,128)(2,1)S(1)} %slice.177), channel_id=1, source_target_pairs={{0,32},{16,48},{32,0},{48,16},{1,33},{17,49},{33,1},{49,17},{2,34}... | collective-permute-start | bytes 1179656 | tf_op jit(solution)/shard_map/ppermute | solution.py:27
  178.0 1.0 copy-start.5
Sparse Core Ops, SparseCore 0:
  20.9 77.4 all-gather.1
  101.0 73.6 reduce-scatter.1
